TPU v7x, 256 devices: a whole 4x4x8 slice. The times are simulated.
256 devices in a mesh: grp: 2 (over x_hi), wa: 128 (over z, x_lo, y, core).
Axes of the slice: x: 4 (x_hi: 2, x_lo: 2; x = x_hi * 2 + x_lo), y: 4, z: 8, core: 2. Of those that a mesh axis runs over, the one named last changes fastest.
Arguments:
- table: bfloat16 [1048576, 128], P(('grp', 'wa')), may hold values from -6 to 6
- owners: int32 [2, 16384, 8, 4], P('grp', 'wa'), may hold values from 0 to 127, all different within a row; in each aligned block of 1024 rows (0 to 1023, 1024 to 2047, ..., all dimensions but the last counted through in order) at most 64 rows name the same one
- local_rows: int32 [2, 16384, 8, 4], P('grp', 'wa'), may hold values from 0 to 4095
- lengths: int32 [2, 16384, 8], P('grp', 'wa'), may hold values from 2 to 4
- labels: float32 [16384], P('wa'), may hold values from 0 to 1
- w_first: bfloat16 [2048, 4096], P('grp'), may hold values from -0.125 to 0.125
- w_head: bfloat16 [4096], replicated, may hold values from -0.09375 to 0.09375
Outputs:
- logits: float32 [16384], P('wa')
- dense_grad: float32 [2048, 4096], P(('grp', 'wa'))
- head_grad: float32 [4096], P(('grp', 'wa'))
- row_grad: bfloat16 [1048576, 128], P(('grp', 'wa'))
Inputs may be any that keep to these rules, and one draw needn't show every extreme that they name: Within the 1024 bags of one device's samples, each owner is named at most 64 times, a bound that some block reaches; the 4 owners of one bag differ.
All inputs are finite; a program needn't handle non-finite values.
Results may differ from a plain program's by a relative error of at most 0.007.
Values may be sent and summed in bfloat16 or wider, within the bound.
No kernel may reach another device: no remote copies, remote signals or barrier semaphores. Data moves between devices by JAX's collectives and lax.ppermute only.
A program may use at most 128 MiB of HBM per device.

v0:
```python
import functools

import jax
import jax.numpy as jnp
from jax import lax
from jax.experimental import pallas as pl
from jax.experimental.pallas import tpu as pltpu
from jax.sharding import PartitionSpec as P

BF16 = jnp.bfloat16
F32 = jnp.float32
I32 = jnp.int32
E = 128
CAP = 64
ROWS_BITS = 12
LOW_BITS = 9
LOW = 1 << LOW_BITS
NT = (((1,), (1,)), ((), ()))


def one_hot(left, right):
    return jnp.where(left == right, 1.0, 0.0).astype(BF16)


def route_kernel(code_ref, ids_ref, bag_ref, bag_t_ref):
    lines = code_ref.shape[0]
    owners = ids_ref.shape[0]
    pairs = owners // 2
    features = lines // 4
    sub = lax.broadcasted_iota(I32, (owners, E), 0)
    half_sub = lax.broadcasted_iota(I32, (CAP, E), 0)
    pair_sub = lax.broadcasted_iota(I32, (pairs, E), 0)
    lane = lax.broadcasted_iota(I32, (1, E), 1)
    before = one_hot(
        jnp.where(lax.broadcasted_iota(I32, (E, E), 0) < lax.broadcasted_iota(I32, (E, E), 1), 1, 0), 1
    )
    named = [jnp.where(sub == code_ref[k : k + 1, :] >> ROWS_BITS, 1.0, 0.0) for k in range(lines)]
    carry = jnp.zeros((owners, 1), F32)
    ids = jnp.zeros((owners, 2 * CAP), F32)
    bag = jnp.zeros((pairs, 2 * E), F32)
    together = 4
    for start in range(0, lines, together):
        owner_parts, place_parts, pair_parts, spot_parts = [], [], [], []
        for k in range(start, start + together):
            code = code_ref[k : k + 1, :]
            owner = code >> ROWS_BITS
            local = code & ((1 << ROWS_BITS) - 1)
            number = (k % features) * E + lane + 1
            named_b = named[k].astype(BF16)
            rank = jnp.dot(named_b, before, preferred_element_type=F32) + carry
            carry = carry + jnp.sum(named[k], axis=1, keepdims=True)
            position = jnp.sum(named[k] * rank, axis=0, keepdims=True).astype(I32)
            place = half_sub == position
            spot = sub == (owner & 1) * CAP + position
            owner_parts.append(named_b)
            place_parts.append(
                jnp.concatenate(
                    [jnp.where(place, (local >> 6).astype(F32), 0.0), jnp.where(place, (local & 63).astype(F32), 0.0)],
                    axis=0,
                ).astype(BF16)
            )
            pair_parts.append(one_hot(pair_sub, owner >> 1))
            spot_parts.append(
                jnp.concatenate(
                    [jnp.where(spot, (number >> 5).astype(F32), 0.0), jnp.where(spot, (number & 31).astype(F32), 0.0)],
                    axis=0,
                ).astype(BF16)
            )
        join = functools.partial(jnp.concatenate, axis=1)
        ids += lax.dot_general(join(owner_parts), join(place_parts), NT, preferred_element_type=F32)
        bag += lax.dot_general(join(pair_parts), join(spot_parts), NT, preferred_element_type=F32)
    ids_ref[...] = (ids[:, :CAP] * 64.0 + ids[:, CAP:]).astype(I32)
    bag = bag[:, :E] * 32.0 + bag[:, E:] - 1.0
    bag_ref[...] = bag.astype(I32)
    bag_t_ref[...] = jnp.transpose(bag).astype(I32)


def spread_columns(lists_t, rows, out_ref):
    for c in range(lists_t.shape[1]):
        out_ref[c * rows : (c + 1) * rows, :] = jnp.broadcast_to(lists_t[:, c : c + 1], (rows, E))


def by_high(data, wide_ref):
    for h in range(data.shape[0] // LOW):
        wide_ref[:, h * E : (h + 1) * E] = data[h * LOW : (h + 1) * LOW, :]


def pick_rows(wanted_ref, wide_ref, out_ref, block):
    lane = lax.broadcasted_iota(I32, (1, E), 1)

    def body(i, _):
        start = pl.multiple_of(i * block, block)
        wanted = wanted_ref[pl.ds(start, block), :]
        low = wanted & (LOW - 1)
        high = wanted >> LOW_BITS
        left = jnp.concatenate([one_hot(low, lane + m * E) for m in range(LOW // E)], axis=1)
        total = jnp.zeros((block, E), F32)
        for h in range(0, wide_ref.shape[1] // E, 2):
            both = jnp.dot(left, wide_ref[:, h * E : (h + 2) * E], preferred_element_type=F32)
            total = jnp.where(high == h, both[:, :E], total)
            total = jnp.where(high == h + 1, both[:, E:], total)
        out_ref[pl.ds(start, block), :] = total.astype(BF16)
        return 0

    lax.fori_loop(0, out_ref.shape[0] // block, body, 0)


def sum_rows(lists_ref, high_ref, data_ref, total_ref):
    chunk = 8
    size = chunk * E
    sub = lax.broadcasted_iota(I32, (LOW, E), 0)
    total_ref[...] = jnp.zeros_like(total_ref)

    def body(i, _):
        start = pl.multiple_of(i * size, size)
        lists = lists_ref[pl.ds(pl.multiple_of(i * chunk, chunk), chunk), :] & (LOW - 1)
        left = jnp.concatenate([one_hot(sub, lists[m : m + 1, :]) for m in range(chunk)], axis=1)
        high = high_ref[pl.ds(start, size), :]
        data = data_ref[pl.ds(start, size), :]
        for h in range(0, total_ref.shape[1] // E, 2):
            right = jnp.concatenate(
                [jnp.where(high == jnp.array(g, BF16), data, jnp.array(0, BF16)) for g in (h, h + 1)], axis=1
            )
            total_ref[:, h * E : (h + 2) * E] += jnp.dot(left, right, preferred_element_type=F32)
        return 0

    lax.fori_loop(0, lists_ref.shape[0] // chunk, body, 0)


def gather_kernel(ids_ref, table_ref, out_ref, spread, wide):
    ids_t = jnp.transpose(ids_ref[...].astype(F32)).astype(I32)
    spread_columns(ids_t, CAP, spread)
    by_high(table_ref, wide)
    pick_rows(spread, wide, out_ref, 1024)


def pool_kernel(bag_ref, bag_t_ref, rows_ref, pooled_ref, high, total):
    samples = pooled_ref.shape[0]
    spread_columns((bag_t_ref[...] >> LOW_BITS).astype(F32).astype(BF16), E, high)
    sum_rows(bag_ref, high, rows_ref, total)
    for f in range(pooled_ref.shape[1] // E):
        h, low = divmod(f * samples, LOW)
        pooled_ref[:, f * E : (f + 1) * E] = total[low : low + samples, h * E : (h + 1) * E].astype(BF16)


def part_kernel(pooled_ref, w_ref, part_ref):
    step = 512
    for j in range(w_ref.shape[1] // step):
        part_ref[:, j * step : (j + 1) * step] = jnp.dot(
            pooled_ref[...], w_ref[:, j * step : (j + 1) * step], preferred_element_type=F32
        )


def peer(where_ref, e, sign):
    return (where_ref[1] + sign * (e // 2) + 4) % 4 * 2 + (where_ref[2] + e % 2) % 2


def head_kernel(
    where_ref, part_ref, pooled_ref, w_near_ref, w_far_ref, labels_ref, w_head_ref,
    logits_ref, head_ref, grad_ref, *rest
):
    piece_refs, total = rest[:-1], rest[-1]
    pieces, samples, width = grad_ref.shape
    half = w_near_ref.shape[0]
    near = pooled_ref[:, pl.ds(pl.multiple_of(where_ref[2] * half, half), half)]
    far = pooled_ref[:, pl.ds(pl.multiple_of((1 - where_ref[2]) * half, half), half)]
    logits = jnp.zeros((samples, 1), F32)
    for q in range(pieces):
        cols = slice(q * width, (q + 1) * width)
        pre = part_ref[:, cols] + (
            jnp.dot(near, w_near_ref[:, cols], preferred_element_type=F32)
            + jnp.dot(far, w_far_ref[:, cols], preferred_element_type=F32)
        )
        total[:, cols] = pre
        hidden = (pre * jax.nn.sigmoid(pre)).astype(BF16).astype(F32)
        logits += jnp.sum(hidden * w_head_ref[:, cols].astype(F32), axis=1, keepdims=True)
    logits_ref[...] = logits
    dlogit = jax.nn.sigmoid(logits) - labels_ref[...]
    for q in range(pieces):
        cols = slice(q * width, (q + 1) * width)
        pre = total[:, cols]
        gate = jax.nn.sigmoid(pre)
        hidden = (pre * gate).astype(BF16).astype(F32)
        head_ref[:, cols] = jnp.sum(hidden * dlogit, axis=0, keepdims=True)
        slope = gate * (1.0 + pre * (1.0 - gate))
        grad_ref[q] = (dlogit * w_head_ref[:, cols].astype(F32) * slope).astype(BF16)
    for e in range(pieces):
        piece_refs[e][...] = grad_ref[peer(where_ref, e, 1)]


def back_kernel(grad_ref, w_ref, bag_t_ref, out_ref, spread, wide):
    pieces, samples, width = grad_ref.shape
    half = w_ref.shape[0] // 2
    spread_columns(bag_t_ref[...], E, spread)
    for h in range(2):
        total = jnp.zeros((samples, half), F32)
        for q in range(pieces):
            total += lax.dot_general(
                grad_ref[q],
                w_ref[h * half : (h + 1) * half, q * width : (q + 1) * width],
                NT,
                preferred_element_type=F32,
            )
        for f in range(half // E):
            high, low = divmod((h * (half // E) + f) * samples, LOW)
            wide[low : low + samples, high * E : (high + 1) * E] = total[:, f * E : (f + 1) * E].astype(BF16)
    pick_rows(spread, wide, out_ref, 1024)


def dense_kernel(where_ref, head_ref, *refs):
    feature_refs, grad_refs, (mine_ref, head_mine_ref, send_ref) = refs[:8], refs[8:16], refs[16:]
    left = jnp.concatenate([r[...] for r in feature_refs], axis=0)
    right = jnp.concatenate([r[...] for r in grad_refs], axis=0)
    half, width = mine_ref.shape[1:]
    planes = mine_ref.shape[0]
    own = where_ref[3] == 0
    share = planes * 2 * E
    head = head_ref[:, pl.ds(pl.multiple_of(where_ref[4] * share, share), share)]
    lines = [head[:, k * E : (k + 1) * E] for k in range(2 * planes)]
    first, second = jnp.concatenate(lines[0::2], axis=0), jnp.concatenate(lines[1::2], axis=0)
    head_mine_ref[...] = jnp.where(own, first, second)
    away = jnp.where(own, second, first)
    high = away.astype(BF16).astype(F32)
    tail = jnp.concatenate([high, away - high], axis=0).astype(BF16)
    send_ref[planes * half :, :] = jnp.concatenate([tail] * (width // E), axis=1)
    for z in range(planes):
        both = lax.dot_general(
            left[:, 2 * half * z : 2 * half * (z + 1)], right, (((0,), (0,)), ((), ())), preferred_element_type=F32
        )
        mine_ref[z] = jnp.where(own, both[:half], both[half:])
        send_ref[z * half : (z + 1) * half, :] = jnp.where(own, both[half:], both[:half]).astype(BF16)


def cross_kernel(mine_ref, head_ref, theirs_ref, out_ref):
    planes, half, width = mine_ref.shape
    rows = half // 8
    tail = theirs_ref[planes * half :, :E].astype(F32)
    head = head_ref[...] + tail[:planes] + tail[planes:]
    high = head.astype(BF16).astype(F32)
    rest = head - high
    empty = jnp.zeros((6, E), F32)
    for z in range(planes):
        block = mine_ref[z] + theirs_ref[z * half : (z + 1) * half, :].astype(F32)
        last = jnp.concatenate([high[z : z + 1], rest[z : z + 1], empty], axis=0)
        parts = []
        for q in range(8):
            parts += [block[q * rows : (q + 1) * rows, m * E : (m + 1) * E] for m in range(width // E)] + [last]
        size = 8 * rows * (width // E + 1)
        out_ref[z * size : (z + 1) * size, :] = jnp.concatenate(parts, axis=0).astype(BF16)


def final_kernel(data_ref, dense_ref, head_ref):
    width = dense_ref.shape[1] // 8
    tiles = width // E
    size = 8 * (tiles + 1)
    head = jnp.zeros((8, E), F32)
    for q in range(0, 8, 2):
        total = jnp.zeros((2 * size, E), F32)
        for z in range(8):
            start = (z * 8 + q) * size
            total += data_ref[start : start + 2 * size, :].astype(F32)
        for n in range(2):
            for m in range(tiles):
                low = n * size + m * 8
                column = (q + n) * width + m * E
                dense_ref[:, column : column + E] = total[low : low + 8]
            head += total[n * size + tiles * 8 : (n + 1) * size]
    head_ref[...] = head[0:1] + head[1:2]


def scatter_kernel(ids_ref, ids2_ref, data_ref, out_ref, high, total):
    ids_t = jnp.transpose((ids_ref[...] >> LOW_BITS).astype(F32)).astype(BF16)
    spread_columns(ids_t, CAP, high)
    sum_rows(ids2_ref, high, data_ref, total)
    for h in range(out_ref.shape[0] // LOW):
        out_ref[h * LOW : (h + 1) * LOW, :] = total[:, h * E : (h + 1) * E].astype(BF16)


def call(kernel, outs, flops, moved, scratch=(), placed=None, mib=16):
    specs = {}
    if placed is not None:
        specs["in_specs"] = [pl.BlockSpec(memory_space=pltpu.SMEM)] + [pl.BlockSpec(memory_space=pltpu.VMEM)] * placed
    return pl.pallas_call(
        kernel,
        out_shape=outs,
        **specs,
        scratch_shapes=list(scratch),
        compiler_params=pltpu.CompilerParams(vmem_limit_bytes=mib << 20),
        cost_estimate=pl.CostEstimate(flops=flops, bytes_accessed=moved, transcendentals=0),
    )


def shape(dims, kind):
    return jax.ShapeDtypeStruct(dims, kind)


def shards(table, owners, local_rows, lengths, labels, w_first, w_head):
    count = lax.axis_size("wa")
    samples = labels.shape[0]
    bags_here = owners.shape[2]
    depth = owners.shape[3]
    hidden_width = w_head.shape[0]
    feats = bags_here * E
    slots = count * CAP
    bags = samples * bags_here
    place = lax.axis_index("wa")
    group = lax.axis_index("grp")
    y = (place // 2) % 4
    core = place % 2
    x_low = (place // 8) % 2

    where = jnp.stack([place // 16, y, core, x_low, group]).astype(I32)

    def moved(step):
        def target(w):
            z, x, yy, c = step(w // 16, (w // 8) % 2, (w // 2) % 4, w % 2)
            return ((z % 8 * 2 + x % 2) * 4 + yy % 4) * 2 + c % 2

        return [(w, target(w)) for w in range(count)]

    to_x = moved(lambda z, x, yy, c: (z, 1 - x, yy, c))
    to_peer = [moved(lambda z, x, yy, c, e=e: (z, x, yy + e // 2, c + e % 2)) for e in range(8)]
    across = [(g * count + w, (1 - g) * count + t) for g in range(2) for w, t in to_x]
    groups = [[z * 16 + x * 8 + r for z in range(8) for r in range(8)] for x in range(2)]

    live = jnp.arange(depth, dtype=I32) < lengths[0][:, :, None]
    code = jnp.where(live, owners[0] * (1 << ROWS_BITS) + local_rows[0], -1)
    code = jnp.transpose(code, (2, 1, 0)).reshape(depth * bags_here, samples)
    ids, bag, bag_t = call(
        route_kernel,
        (shape((count, CAP), I32), shape((count // 2, 2 * CAP), I32), shape((2 * CAP, count // 2), I32)),
        2 * 4096 * 128 * 1024,
        100000,
    )(code)
    ids, w_early = lax.optimization_barrier((ids, w_first))
    near_half = lax.dynamic_slice_in_dim(w_early, core * (feats // 2), feats // 2)
    near_half = lax.ppermute(near_half, ("grp", "wa"), across)
    far_half = lax.ppermute(near_half, "wa", to_peer[1])
    ids_in = lax.all_to_all(ids, "wa", split_axis=0, concat_axis=0, tiled=True)
    tiles = call(
        gather_kernel,
        shape((slots, E), BF16),
        2 * slots * 4096 * E,
        4 << 20,
        [pltpu.VMEM((slots, E), I32), pltpu.VMEM((LOW, table.shape[0] // LOW * E), BF16)],
    )(ids_in, table)
    returned = lax.all_to_all(
        tiles.reshape(count, CAP, E), "wa", split_axis=0, concat_axis=0, tiled=True
    ).reshape(slots, E)
    pooled = call(
        pool_kernel,
        shape((samples, feats), BF16),
        2 * slots * 1024 * E,
        4 << 20,
        [pltpu.VMEM((slots, E), BF16), pltpu.VMEM((LOW, bags // LOW * E), F32)],
    )(bag, bag_t, returned)
    other = lax.ppermute(pooled, "grp", [(0, 1), (1, 0)])
    part = call(
        part_kernel, shape((samples, hidden_width), F32), 2 * samples * feats * hidden_width, 10 << 20, mib=20
    )(pooled, w_first)

    side_pooled = [lax.ppermute(pooled, "wa", to_peer[2 * d]) for d in range(1, 4)]

    width = hidden_width // 8
    logits, head, grad, *pieces = call(
        head_kernel,
        (
            shape((samples, 1), F32),
            shape((1, hidden_width), F32),
            shape((8, samples, width), BF16),
        )
        + (shape((samples, width), BF16),) * 8,
        2 * samples * feats * hidden_width + samples * hidden_width * 60,
        4 << 20,
        [pltpu.VMEM((samples, hidden_width), F32)],
        placed=6,
        mib=24,
    )(where, part, other, near_half, far_half, labels.reshape(samples, 1), w_head.reshape(1, hidden_width))

    grad, *side_pooled = lax.optimization_barrier((grad, *side_pooled))
    all_pooled = []
    for value in [pooled] + side_pooled:
        all_pooled += [value, lax.ppermute(value, "wa", to_peer[1])]

    send = call(
        back_kernel,
        shape((slots, E), BF16),
        2 * slots * 1024 * E + 2 * samples * feats * hidden_width,
        12 << 20,
        [pltpu.VMEM((slots, E), I32), pltpu.VMEM((LOW, bags // LOW * E), BF16)],
        mib=24,
    )(grad, w_first, bag_t)
    send, *pieces = lax.optimization_barrier((send, *pieces))
    arrived = lax.all_to_all(
        send.reshape(count, CAP, E), "wa", split_axis=0, concat_axis=0, tiled=True
    ).reshape(slots, E)

    grads = pieces[:1] + [lax.ppermute(pieces[e], "wa", to_peer[e]) for e in range(1, 8)]
    planes = count // 16
    half = feats // planes // 2
    mine, head_mine, theirs = call(
        dense_kernel,
        (
            shape((planes, half, width), F32),
            shape((planes, E), F32),
            shape((planes * half + 16, width), BF16),
        ),
        2 * feats * width * 8 * samples,
        8 << 20,
        placed=17,
    )(where, head, *all_pooled, *grads)
    theirs = lax.ppermute(theirs, "wa", to_x)
    size = half // 8 * (width // E + 1)
    laid = call(cross_kernel, shape((8 * planes * size, E), BF16), 1 << 20, 2 << 20)(mine, head_mine, theirs)
    other_logits = lax.ppermute(logits, "grp", [(0, 1), (1, 0)])
    laid, ids_pairs, other_logits, arrived = lax.optimization_barrier(
        (laid, ids_in.reshape(count // 2, 2 * CAP), other_logits, arrived)
    )
    blocks = lax.all_to_all(
        laid.reshape(8 * planes, size, E), "wa", 0, 0, axis_index_groups=groups, tiled=True
    ).reshape(8 * planes * size, E)
    dense_grad, head_sums = call(
        final_kernel, (shape((8, hidden_width), F32), shape((1, E), F32)), 1 << 20, 1 << 20
    )(blocks)
    head_grad = lax.dynamic_index_in_dim(head_sums.reshape(8, E // 8), place % 8, 0, False)

    row_grad = call(
        scatter_kernel,
        shape((table.shape[0], E), BF16),
        2 * slots * 4096 * E,
        4 << 20,
        [pltpu.VMEM((slots, E), BF16), pltpu.VMEM((LOW, table.shape[0] // LOW * E), F32)],
    )(ids_in, ids_pairs, arrived)
    logits = jnp.where(group == 0, logits, other_logits)
    return (logits.reshape(samples), dense_grad, head_grad, row_grad)


def solution(mesh):
    return jax.shard_map(
        shards,
        mesh=mesh,
        in_specs=(
            P(("grp", "wa"), None),
            P("grp", "wa", None, None),
            P("grp", "wa", None, None),
            P("grp", "wa", None),
            P("wa"),
            P("grp", None),
            P(),
        ),
        out_specs=(P("wa"), P(("grp", "wa"), None), P(("grp", "wa")), P(("grp", "wa"), None)),
        check_vma=False,
    )
```

profile of v0, /device:TPU:1, one launch (start us, length us, event | category | flops | bytes accessed | tf_op | source)
XLA Modules:
  0.0 243.4 jit_solution(13522974513703539260)
XLA Ops:
  1.4 2.4 %shard_map.102 = (s32[128,64]{1,0:T(8,128)S(1)}, s32[64,128]{1,0:T(8,128)S(1)}, s32[128,64]{1,0:T(8,128)S(1)}) custom-call(s32[32,128]{1,0:T(8,128)S(1)} %bitcast.38), custom_call_target="tpu_custom_call" | custom-call | flops 1073741824 | bytes 100000 | tf_op jit(solution)/shard_map/pallas_call | solution.py:329
  3.9 4.8 %constant_dynamic-slice_fusion = bf16[512,4096]{1,0:T(8,128)(2,1)} fusion(bf16[1024,4096]{1,0:T(8,128)(2,1)} %w_ref.3, s32[]{:T(128)S(6)} %select_n.56), kind=kLoop, calls=%fused_computation.6 | loop fusion | bytes 8388612 | tf_op jit(solution)/shard_map/dynamic_slice | solution.py:336
  8.7 3.3 %collective-permute-start.1 = (bf16[512,4096]{1,0:T(8,128)(2,1)}, bf16[512,4096]{1,0:T(8,128)(2,1)}, u32[]{:S(2)}, u32[]{:S(2)}) collective-permute-start(bf16[512,4096]{1,0:T(8,128)(2,1)} %constant_dynamic-slice_fusion), channel_id=1, source_target_pairs={{0,136},{1,137},{2,138},{3,139},{4,140},{5,141},{6,142},{7,143},{8... | collective-permute-start | bytes 12582920 | tf_op jit(solution)/shard_map/ppermute | solution.py:337
  12.0 23.8 %all_to_all.26 = s32[128,1,64]{2,1,0:T(1,128)S(1)} all-to-all(s32[128,1,64]{2,1,0:T(1,128)S(1)} %bitcast.37), channel_id=1, replica_groups=mesh['grp'=2,'wa'=128] {'wa'}, dimensions={0} | all-to-all | bytes 65536 | tf_op jit(solution)/shard_map/all_to_all | solution.py:339
  35.8 11.5 %shard_map.103 = bf16[8192,128]{1,0:T(8,128)(2,1)S(1)} custom-call(s32[128,64]{1,0:T(8,128)S(1)} %bitcast.35, bf16[4096,128]{1,0:T(8,128)(2,1)S(1)} %copy-done.3), custom_call_target="tpu_custom_call" | custom-call | flops 8589934592 | bytes 4194304 | tf_op jit(solution)/shard_map/pallas_call | solution.py:340
  48.6 5.9 %all-to-all-start.1 = ((bf16[128,64,128]{2,1,0:T(8,128)(2,1)}), bf16[128,64,128]{2,1,0:T(8,128)(2,1)S(1)}, u32[]{:S(2)}, u32[]{:S(2)}) async-start(bf16[128,64,128]{2,1,0:T(8,128)(2,1)} %bitcast.34), calls=%async_computation.1 | async-start | bytes 4194304 | tf_op jit(solution)/shard_map/all_to_all | solution.py:347
  54.5 47.0 %collective-permute-done.1.w_near_ref = bf16[512,4096]{1,0:T(8,128)(2,1)} collective-permute-done((bf16[512,4096]{1,0:T(8,128)(2,1)}, bf16[512,4096]{1,0:T(8,128)(2,1)}, u32[]{:S(2)}, u32[]{:S(2)}) %collective-permute-start.1) | collective-permute-done | bytes 4194336 | tf_op jit(solution)/shard_map/ppermute | solution.py:337
  101.6 2.3 collective-permute-start.2
  106.0 4.5 %shard_map.104.pooled_ref.refs_0_ = bf16[128,1024]{1,0:T(8,128)(2,1)S(1)} custom-call(s32[64,128]{1,0:T(8,128)S(1)} %get-tuple-element.42.bag_ref, s32[128,64]{1,0:T(8,128)S(1)} %get-tuple-element.43.bag_t_ref, bf16[8192,128]{1,0:T(8,128)(2,1)S(1)} %bitcast.33), custom_call_target="tpu_custom_call" | custom-call | flops 2147483648 | bytes 4194304 | tf_op jit(solution)/shard_map/pallas_call | solution.py:350
  111.8 2.8 %collective-permute-start.5 = (bf16[128,1024]{1,0:T(8,128)(2,1)S(1)}, bf16[128,1024]{1,0:T(8,128)(2,1)S(1)}, u32[]{:S(2)}, u32[]{:S(2)}) collective-permute-start(bf16[128,1024]{1,0:T(8,128)(2,1)S(1)} %shard_map.104.pooled_ref.refs_0_), channel_id=1, source_target_pairs={{0,4},{1,5},{2,6},{3,7},{4,0},{5,1},{6,2},{7,3},{8,12},{9,13},{10,... | collective-permute-start | bytes 786440 | tf_op jit(solution)/shard_map/ppermute | solution.py:362
  115.7 3.4 %copy-done = bf16[1024,4096]{1,0:T(8,128)(2,1)S(1)} copy-done((bf16[1024,4096]{1,0:T(8,128)(2,1)S(1)}, bf16[1024,4096]{1,0:T(8,128)(2,1)}, u32[]{:S(2)}) %copy-start) | copy-done | bytes 8388632
  120.4 6.0 %shard_map.106 = (f32[128,1]{1,0:T(8,128)S(1)}, f32[1,4096]{1,0:T(1,128)S(1)}, bf16[8,128,512]{2,1,0:T(8,128)(2,1)S(1)}, bf16[128,512]{1,0:T(8,128)(2,1)S(1)}, b...) custom-call(s32[5]{0:T(128)S(1)} %stack.23.where_ref, ...), custom_call_target="tpu_custom_call" | custom-call | flops 1105199104 | bytes 4194304 | tf_op jit(solution)/shard_map/pallas_call | solution.py:365
  126.6 6.4 %shard_map.107 = bf16[8192,128]{1,0:T(8,128)(2,1)S(1)} custom-call(bf16[8,128,512]{2,1,0:T(8,128)(2,1)S(1)} %get-tuple-element.53.grad_ref, bf16[1024,4096]{1,0:T(8,128)(2,1)S(1)} %bitcast.29, s32[128,64]{1,0:T(8,128)S(1)} %copy-done.20), custom_call_target="tpu_custom_call" | custom-call | flops 3221225472 | bytes 12582912 | tf_op jit(solution)/shard_map/pallas_call | solution.py:385
  134.4 13.4 %all-to-all-start.2 = ((bf16[128,64,128]{2,1,0:T(8,128)(2,1)}), bf16[128,64,128]{2,1,0:T(8,128)(2,1)S(1)}, u32[]{:S(2)}, u32[]{:S(2)}) async-start(bf16[128,64,128]{2,1,0:T(8,128)(2,1)} %bitcast.32), calls=%async_computation.2 | async-start | bytes 4194304 | tf_op jit(solution)/shard_map/all_to_all | solution.py:394
  154.9 4.3 %collective-permute-done.11.refs_10_ = bf16[128,512]{1,0:T(8,128)(2,1)S(1)} collective-permute-done((bf16[128,512]{1,0:T(8,128)(2,1)}, bf16[128,512]{1,0:T(8,128)(2,1)S(1)}, u32[]{:S(2)}, u32[]{:S(2)}) %collective-permute-start.11) | collective-permute-done | bytes 131104 | tf_op jit(solution)/shard_map/ppermute | solution.py:398
  159.9 3.9 %collective-permute-done.12.refs_11_ = bf16[128,512]{1,0:T(8,128)(2,1)S(1)} collective-permute-done((bf16[128,512]{1,0:T(8,128)(2,1)}, bf16[128,512]{1,0:T(8,128)(2,1)S(1)}, u32[]{:S(2)}, u32[]{:S(2)}) %collective-permute-start.12) | collective-permute-done | bytes 131104 | tf_op jit(solution)/shard_map/ppermute | solution.py:398
  164.1 5.2 %collective-permute-done.13.refs_12_ = bf16[128,512]{1,0:T(8,128)(2,1)S(1)} collective-permute-done((bf16[128,512]{1,0:T(8,128)(2,1)}, bf16[128,512]{1,0:T(8,128)(2,1)S(1)}, u32[]{:S(2)}, u32[]{:S(2)}) %collective-permute-start.13) | collective-permute-done | bytes 131104 | tf_op jit(solution)/shard_map/ppermute | solution.py:398
  169.4 5.4 %collective-permute-done.14.refs_13_ = bf16[128,512]{1,0:T(8,128)(2,1)S(1)} collective-permute-done((bf16[128,512]{1,0:T(8,128)(2,1)}, bf16[128,512]{1,0:T(8,128)(2,1)S(1)}, u32[]{:S(2)}, u32[]{:S(2)}) %collective-permute-start.14) | collective-permute-done | bytes 131104 | tf_op jit(solution)/shard_map/ppermute | solution.py:398
  175.8 8.4 %collective-permute-done.16.refs_15_ = bf16[128,512]{1,0:T(8,128)(2,1)S(1)} collective-permute-done((bf16[128,512]{1,0:T(8,128)(2,1)S(1)}, bf16[128,512]{1,0:T(8,128)(2,1)S(1)}, u32[]{:S(2)}, u32[]{:S(2)}) %collective-permute-start.16) | collective-permute-done | bytes 131104 | tf_op jit(solution)/shard_map/ppermute | solution.py:398
  188.7 2.6 %shard_map.108 = (f32[8,64,512]{2,1,0:T(8,128)S(1)}, f32[8,128]{1,0:T(8,128)S(1)}, bf16[528,512]{1,0:T(8,128)(2,1)}) custom-call(s32[5]{0:T(128)S(1)} %stack.23.where_ref, f32[1,4096]{1,0:T(1,128)S(1)} %copy-done.18, bf16[128,1024]{1,0:T(8,128)(2,1)S(1)} %shard_map.104.pooled_ref.refs_0_, bf16[128,1024]{1,0:T(8,128)(2,1)S(1)} %collective-permute-done.3.refs_1_, ...), custom_call_target="tpu_custom_call" | custom-call | flops 1073741824 | bytes 8388608 | tf_op jit(solution)/shard_map/pallas_call | solution.py:401
  193.6 12.8 %collective-permute-done.17.theirs_ref = bf16[528,512]{1,0:T(8,128)(2,1)} collective-permute-done((bf16[528,512]{1,0:T(8,128)(2,1)}, bf16[528,512]{1,0:T(8,128)(2,1)}, u32[]{:S(2)}, u32[]{:S(2)}) %collective-permute-start.17) | collective-permute-done | bytes 540704 | tf_op jit(solution)/shard_map/ppermute | solution.py:412
  208.4 12.2 %all-to-all-start.3 = ((bf16[64,40,128]{2,1,0:T(8,128)(2,1)}), bf16[64,40,128]{2,1,0:T(8,128)(2,1)S(1)}, u32[]{:S(2)}, u32[]{:S(2)}) async-start(bf16[64,40,128]{2,1,0:T(8,128)(2,1)} %bitcast.17), calls=%async_computation.3 | async-start | bytes 1310720 | tf_op jit(solution)/shard_map/all_to_all | solution.py:419
  221.2 12.5 %shard_map.111 = bf16[4096,128]{1,0:T(8,128)(2,1)} custom-call(s32[128,64]{1,0:T(8,128)S(1)} %bitcast.36, s32[64,128]{1,0:T(8,128)S(1)} %reshape.56.ids2_ref, bf16[8192,128]{1,0:T(8,128)(2,1)S(1)} %bitcast.31), custom_call_target="tpu_custom_call" | custom-call | flops 8589934592 | bytes 4194304 | tf_op jit(solution)/shard_map/pallas_call | solution.py:427
  233.7 7.2 %all-to-all-done.3 = bf16[64,40,128]{2,1,0:T(8,128)(2,1)S(1)} async-done(((bf16[64,40,128]{2,1,0:T(8,128)(2,1)}), bf16[64,40,128]{2,1,0:T(8,128)(2,1)S(1)}, u32[]{:S(2)}, u32[]{:S(2)}) %all-to-all-start.3) | async-done | bytes 655392 | tf_op jit(solution)/shard_map/all_to_all | solution.py:419
  (96 shorter events, 30.4 us)
Async XLA Ops:
  3.9 102.1 %copy-start.19 = (s32[128,64]{1,0:T(8,128)}, s32[128,64]{1,0:T(8,128)S(1)}, u32[]{:S(2)}) copy-start(s32[128,64]{1,0:T(8,128)S(1)} %get-tuple-element.43.bag_t_ref) | copy-start | bytes 98308
  8.7 92.9 %collective-permute-start.1 = (bf16[512,4096]{1,0:T(8,128)(2,1)}, bf16[512,4096]{1,0:T(8,128)(2,1)}, u32[]{:S(2)}, u32[]{:S(2)}) collective-permute-start(bf16[512,4096]{1,0:T(8,128)(2,1)} %constant_dynamic-slice_fusion), channel_id=1, source_target_pairs={{0,136},{1,137},{2,138},{3,139},{4,140},{5,141},{6,142},{7,143},{8... | collective-permute-start | bytes 12582920 | tf_op jit(solution)/shard_map/ppermute | solution.py:337
  48.6 57.4 %all-to-all-start.1 = ((bf16[128,64,128]{2,1,0:T(8,128)(2,1)}), bf16[128,64,128]{2,1,0:T(8,128)(2,1)S(1)}, u32[]{:S(2)}, u32[]{:S(2)}) async-start(bf16[128,64,128]{2,1,0:T(8,128)(2,1)} %bitcast.34), calls=%async_computation.1 | async-start | bytes 4194304 | tf_op jit(solution)/shard_map/all_to_all | solution.py:347
  54.5 61.1 %copy-start.21 = (bf16[4096]{0:T(1024)(128)(2,1)S(1)}, bf16[4096]{0:T(1024)(128)(2,1)}, u32[]{:S(2)}) copy-start(bf16[4096]{0:T(1024)(128)(2,1)} %param.13) | copy-start | bytes 24580
  101.6 18.9 %collective-permute-start.2 = (bf16[512,4096]{1,0:T(8,128)(2,1)}, bf16[512,4096]{1,0:T(8,128)(2,1)}, u32[]{:S(2)}, u32[]{:S(2)}) collective-permute-start(bf16[512,4096]{1,0:T(8,128)(2,1)} %collective-permute-done.1.w_near_ref), channel_id=1, source_target_pairs={{0,1},{1,0},{2,3},{3,2},{4,5},{5,4},{6,7},{7,6},{8,9},{9,8},{10,11... | collective-permute-start | bytes 12582920 | tf_op jit(solution)/shard_map/ppermute | solution.py:338
  110.5 10.0 %collective-permute-start = (bf16[128,1024]{1,0:T(8,128)(2,1)S(1)}, bf16[128,1024]{1,0:T(8,128)(2,1)S(1)}, u32[]{:S(2)}, u32[]{:S(2)}) collective-permute-start(bf16[128,1024]{1,0:T(8,128)(2,1)S(1)} %shard_map.104.pooled_ref.refs_0_), channel_id=1, source_target_pairs={{0,128},{128,0},{1,129},{129,1},{2,130},{130,2},{3,131},{131,3},{4... | collective-permute-start | bytes 786440 | tf_op jit(solution)/shard_map/ppermute | solution.py:357
  111.6 14.9 %collective-permute-start.4 = (bf16[128,1024]{1,0:T(8,128)(2,1)S(1)}, bf16[128,1024]{1,0:T(8,128)(2,1)S(1)}, u32[]{:S(2)}, u32[]{:S(2)}) collective-permute-start(bf16[128,1024]{1,0:T(8,128)(2,1)S(1)} %shard_map.104.pooled_ref.refs_0_), channel_id=1, source_target_pairs={{0,2},{1,3},{2,4},{3,5},{4,6},{5,7},{6,0},{7,1},{8,10},{9,11},{10,... | collective-permute-start | bytes 786440 | tf_op jit(solution)/shard_map/ppermute | solution.py:362
  111.8 14.8 %collective-permute-start.5 = (bf16[128,1024]{1,0:T(8,128)(2,1)S(1)}, bf16[128,1024]{1,0:T(8,128)(2,1)S(1)}, u32[]{:S(2)}, u32[]{:S(2)}) collective-permute-start(bf16[128,1024]{1,0:T(8,128)(2,1)S(1)} %shard_map.104.pooled_ref.refs_0_), channel_id=1, source_target_pairs={{0,4},{1,5},{2,6},{3,7},{4,0},{5,1},{6,2},{7,3},{8,12},{9,13},{10,... | collective-permute-start | bytes 786440 | tf_op jit(solution)/shard_map/ppermute | solution.py:362
  114.6 12.0 %collective-permute-start.6 = (bf16[128,1024]{1,0:T(8,128)(2,1)S(1)}, bf16[128,1024]{1,0:T(8,128)(2,1)S(1)}, u32[]{:S(2)}, u32[]{:S(2)}) collective-permute-start(bf16[128,1024]{1,0:T(8,128)(2,1)S(1)} %shard_map.104.pooled_ref.refs_0_), channel_id=1, source_target_pairs={{0,6},{1,7},{2,0},{3,1},{4,2},{5,3},{6,4},{7,5},{8,14},{9,15},{10,... | collective-permute-start | bytes 786440 | tf_op jit(solution)/shard_map/ppermute | solution.py:362
  134.4 73.9 %all-to-all-start.2 = ((bf16[128,64,128]{2,1,0:T(8,128)(2,1)}), bf16[128,64,128]{2,1,0:T(8,128)(2,1)S(1)}, u32[]{:S(2)}, u32[]{:S(2)}) async-start(bf16[128,64,128]{2,1,0:T(8,128)(2,1)} %bitcast.32), calls=%async_computation.2 | async-start | bytes 4194304 | tf_op jit(solution)/shard_map/all_to_all | solution.py:394
  147.8 5.5 %collective-permute-start.3 = (bf16[128,1024]{1,0:T(8,128)(2,1)S(1)}, bf16[128,1024]{1,0:T(8,128)(2,1)S(1)}, u32[]{:S(2)}, u32[]{:S(2)}) collective-permute-start(bf16[128,1024]{1,0:T(8,128)(2,1)S(1)} %shard_map.104.pooled_ref.refs_0_), channel_id=1, source_target_pairs={{0,1},{1,0},{2,3},{3,2},{4,5},{5,4},{6,7},{7,6},{8,9},{9,8},{10,11... | collective-permute-start | bytes 786440 | tf_op jit(solution)/shard_map/ppermute | solution.py:383
  148.8 5.7 %collective-permute-start.10 = (bf16[128,512]{1,0:T(8,128)(2,1)}, bf16[128,512]{1,0:T(8,128)(2,1)S(1)}, u32[]{:S(2)}, u32[]{:S(2)}) collective-permute-start(bf16[128,512]{1,0:T(8,128)(2,1)} %copy-done.16), channel_id=1, source_target_pairs={{0,1},{1,0},{2,3},{3,2},{4,5},{5,4},{6,7},{7,6},{8,9},{9,8},{10,11... | collective-permute-start | bytes 393224 | tf_op jit(solution)/shard_map/ppermute | solution.py:398
  148.9 10.3 %collective-permute-start.11 = (bf16[128,512]{1,0:T(8,128)(2,1)}, bf16[128,512]{1,0:T(8,128)(2,1)S(1)}, u32[]{:S(2)}, u32[]{:S(2)}) collective-permute-start(bf16[128,512]{1,0:T(8,128)(2,1)} %copy-done.15), channel_id=1, source_target_pairs={{0,2},{1,3},{2,4},{3,5},{4,6},{5,7},{6,0},{7,1},{8,10},{9,11},{10,... | collective-permute-start | bytes 393224 | tf_op jit(solution)/shard_map/ppermute | solution.py:398
  149.8 14.0 %collective-permute-start.12 = (bf16[128,512]{1,0:T(8,128)(2,1)}, bf16[128,512]{1,0:T(8,128)(2,1)S(1)}, u32[]{:S(2)}, u32[]{:S(2)}) collective-permute-start(bf16[128,512]{1,0:T(8,128)(2,1)} %copy-done.14), channel_id=1, source_target_pairs={{0,3},{1,2},{2,5},{3,4},{4,7},{5,6},{6,1},{7,0},{8,11},{9,10},{10,... | collective-permute-start | bytes 393224 | tf_op jit(solution)/shard_map/ppermute | solution.py:398
  151.5 17.8 %collective-permute-start.13 = (bf16[128,512]{1,0:T(8,128)(2,1)}, bf16[128,512]{1,0:T(8,128)(2,1)S(1)}, u32[]{:S(2)}, u32[]{:S(2)}) collective-permute-start(bf16[128,512]{1,0:T(8,128)(2,1)} %copy-done.13), channel_id=1, source_target_pairs={{0,4},{1,5},{2,6},{3,7},{4,0},{5,1},{6,2},{7,3},{8,12},{9,13},{10,... | collective-permute-start | bytes 393224 | tf_op jit(solution)/shard_map/ppermute | solution.py:398
  153.3 21.4 %collective-permute-start.14 = (bf16[128,512]{1,0:T(8,128)(2,1)}, bf16[128,512]{1,0:T(8,128)(2,1)S(1)}, u32[]{:S(2)}, u32[]{:S(2)}) collective-permute-start(bf16[128,512]{1,0:T(8,128)(2,1)} %copy-done.12), channel_id=1, source_target_pairs={{0,5},{1,4},{2,7},{3,6},{4,1},{5,0},{6,3},{7,2},{8,13},{9,12},{10,... | collective-permute-start | bytes 393224 | tf_op jit(solution)/shard_map/ppermute | solution.py:398
  154.5 29.6 %collective-permute-start.7 = (bf16[128,1024]{1,0:T(8,128)(2,1)S(1)}, bf16[128,1024]{1,0:T(8,128)(2,1)S(1)}, u32[]{:S(2)}, u32[]{:S(2)}) collective-permute-start(bf16[128,1024]{1,0:T(8,128)(2,1)S(1)} %collective-permute-done.4.refs_2_), channel_id=1, source_target_pairs={{0,1},{1,0},{2,3},{3,2},{4,5},{5,4},{6,7},{7,6},{8,9},{9,8},{10,11... | collective-permute-start | bytes 786440 | tf_op jit(solution)/shard_map/ppermute | solution.py:383
  159.2 25.0 %collective-permute-start.8 = (bf16[128,1024]{1,0:T(8,128)(2,1)S(1)}, bf16[128,1024]{1,0:T(8,128)(2,1)S(1)}, u32[]{:S(2)}, u32[]{:S(2)}) collective-permute-start(bf16[128,1024]{1,0:T(8,128)(2,1)S(1)} %collective-permute-done.5.refs_4_), channel_id=1, source_target_pairs={{0,1},{1,0},{2,3},{3,2},{4,5},{5,4},{6,7},{7,6},{8,9},{9,8},{10,11... | collective-permute-start | bytes 786440 | tf_op jit(solution)/shard_map/ppermute | solution.py:383
  163.8 20.4 %collective-permute-start.9 = (bf16[128,1024]{1,0:T(8,128)(2,1)S(1)}, bf16[128,1024]{1,0:T(8,128)(2,1)S(1)}, u32[]{:S(2)}, u32[]{:S(2)}) collective-permute-start(bf16[128,1024]{1,0:T(8,128)(2,1)S(1)} %collective-permute-done.6.refs_6_), channel_id=1, source_target_pairs={{0,1},{1,0},{2,3},{3,2},{4,5},{5,4},{6,7},{7,6},{8,9},{9,8},{10,11... | collective-permute-start | bytes 786440 | tf_op jit(solution)/shard_map/ppermute | solution.py:383
  169.4 6.4 %collective-permute-start.15 = (bf16[128,512]{1,0:T(8,128)(2,1)S(1)}, bf16[128,512]{1,0:T(8,128)(2,1)S(1)}, u32[]{:S(2)}, u32[]{:S(2)}) collective-permute-start(bf16[128,512]{1,0:T(8,128)(2,1)S(1)} %get-tuple-element.68), channel_id=1, source_target_pairs={{0,6},{1,7},{2,0},{3,1},{4,2},{5,3},{6,4},{7,5},{8,14},{9,15},{10,... | collective-permute-start | bytes 393224 | tf_op jit(solution)/shard_map/ppermute | solution.py:398
  174.8 9.4 %collective-permute-start.16 = (bf16[128,512]{1,0:T(8,128)(2,1)S(1)}, bf16[128,512]{1,0:T(8,128)(2,1)S(1)}, u32[]{:S(2)}, u32[]{:S(2)}) collective-permute-start(bf16[128,512]{1,0:T(8,128)(2,1)S(1)} %get-tuple-element.69), channel_id=1, source_target_pairs={{0,7},{1,6},{2,1},{3,0},{4,3},{5,2},{6,5},{7,4},{8,15},{9,14},{10,... | collective-permute-start | bytes 393224 | tf_op jit(solution)/shard_map/ppermute | solution.py:398
  191.3 15.0 %collective-permute-start.17 = (bf16[528,512]{1,0:T(8,128)(2,1)}, bf16[528,512]{1,0:T(8,128)(2,1)}, u32[]{:S(2)}, u32[]{:S(2)}) collective-permute-start(bf16[528,512]{1,0:T(8,128)(2,1)} %get-tuple-element.72), channel_id=1, source_target_pairs={{0,8},{1,9},{2,10},{3,11},{4,12},{5,13},{6,14},{7,15},{8,0},{9,1},... | collective-permute-start | bytes 1622024 | tf_op jit(solution)/shard_map/ppermute | solution.py:412
  191.3 17.0 %collective-permute-start.18 = (f32[128,1]{1,0:T(8,128)S(1)}, f32[128,1]{1,0:T(8,128)S(1)}, u32[]{:S(2)}, u32[]{:S(2)}) collective-permute-start(f32[128,1]{1,0:T(8,128)S(1)} %get-tuple-element.47), channel_id=1, source_target_pairs={{0,128},{128,0},{1,129},{129,1},{2,130},{130,2},{3,131},{131,3},{4... | collective-permute-start | bytes 1544 | tf_op jit(solution)/shard_map/ppermute | solution.py:415
  208.4 32.5 %all-to-all-start.3 = ((bf16[64,40,128]{2,1,0:T(8,128)(2,1)}), bf16[64,40,128]{2,1,0:T(8,128)(2,1)S(1)}, u32[]{:S(2)}, u32[]{:S(2)}) async-start(bf16[64,40,128]{2,1,0:T(8,128)(2,1)} %bitcast.17), calls=%async_computation.3 | async-start | bytes 1310720 | tf_op jit(solution)/shard_map/all_to_all | solution.py:419
  (23 other events, 268.5 us)
where the time goes:
time: 244 us; the launch traced here: 243 us
  waiting for transfers between devices  97.4 us (40%)
  starting transfers between devices  51 us (21%)
  Pallas kernels  50 us (20%)
  blocking collectives  23.8 us (10%)
  local copies, waits for them, and re-layouts  17.3 us (7%)
  other arithmetic  2.84 us (1%)
    ppermute x1, waiting for transfers between devices, shards(): near_half = lax.ppermute(near_half, ('grp', 'wa'), across)  47 us
    ppermute x7, waiting for transfers between devices, shards(): lax.ppermute(pieces[e], 'wa', to_peer[e])  28.2 us
    all_to_all x1, blocking collectives, shards(): ids_in = lax.all_to_all(ids, 'wa', split_axis=0, concat_axis=0, tiled=True)  23.8 us
    all_to_all x1, starting transfers between devices, shards(): lax.all_to_all(send.reshape(count, CAP, E), 'wa', split_axis=0, concat_ax...  13.4 us
    ppermute x1, waiting for transfers between devices, shards(): theirs = lax.ppermute(theirs, 'wa', to_x)  12.8 us
    pallas_call x1, Pallas kernels, shards(): call(scatter_kernel, shape((table.shape[0], E), BF16), 2 * slots * 4096 *...  12.5 us
    all_to_all x1, starting transfers between devices, shards(): lax.all_to_all(laid.reshape(8 * planes, size, E), 'wa', 0, 0, axis_index_...  12.2 us
    pallas_call x1, Pallas kernels, shards(): call(gather_kernel, shape((slots, E), BF16), 2 * slots * 4096 * E, 4 << 2...  11.5 us
  transfers between devices with their start and end apart: 22, of which 10 were waited for; matrix products, arithmetic and copies ran while one was open for 1% of the time, Pallas kernels for 17%

commit v1 on v0

--- a/solution.py
+++ b/solution.py
@@ -22,11 +22,13 @@
     return jnp.where(left == right, 1.0, 0.0).astype(BF16)
 
 
-def route_kernel(code_ref, ids_ref, bag_ref, bag_t_ref):
+def route_kernel(where_ref, code_ref, w_ref, ids_ref, bag_ref, bag_t_ref, half_ref, sem):
+    rows = half_ref.shape[0]
+    copy = pltpu.make_async_copy(w_ref.at[pl.ds(pl.multiple_of(where_ref[2] * rows, rows), rows), :], half_ref, sem)
+    copy.start()
     lines = code_ref.shape[0]
     owners = ids_ref.shape[0]
     pairs = owners // 2
-    features = lines // 4
     sub = lax.broadcasted_iota(I32, (owners, E), 0)
     half_sub = lax.broadcasted_iota(I32, (CAP, E), 0)
     pair_sub = lax.broadcasted_iota(I32, (pairs, E), 0)
@@ -45,7 +47,7 @@
             code = code_ref[k : k + 1, :]
             owner = code >> ROWS_BITS
             local = code & ((1 << ROWS_BITS) - 1)
-            number = (k % features) * E + lane + 1
+            number = (k // 4) * E + lane + 1
             named_b = named[k].astype(BF16)
             rank = jnp.dot(named_b, before, preferred_element_type=F32) + carry
             carry = carry + jnp.sum(named[k], axis=1, keepdims=True)
@@ -69,10 +71,12 @@
         join = functools.partial(jnp.concatenate, axis=1)
         ids += lax.dot_general(join(owner_parts), join(place_parts), NT, preferred_element_type=F32)
         bag += lax.dot_general(join(pair_parts), join(spot_parts), NT, preferred_element_type=F32)
-    ids_ref[...] = (ids[:, :CAP] * 64.0 + ids[:, CAP:]).astype(I32)
+    ids = ids[:, :CAP] * 64.0 + ids[:, CAP:]
+    ids_ref[...] = jnp.concatenate([ids, ids], axis=1).astype(I32).reshape(ids_ref.shape)
     bag = bag[:, :E] * 32.0 + bag[:, E:] - 1.0
     bag_ref[...] = bag.astype(I32)
     bag_t_ref[...] = jnp.transpose(bag).astype(I32)
+    copy.wait()
 
 
 def spread_columns(lists_t, rows, out_ref):
@@ -105,7 +109,7 @@
     lax.fori_loop(0, out_ref.shape[0] // block, body, 0)
 
 
-def sum_rows(lists_ref, high_ref, data_ref, total_ref):
+def sum_rows(lists, high_ref, data_ref, total_ref):
     chunk = 8
     size = chunk * E
     sub = lax.broadcasted_iota(I32, (LOW, E), 0)
@@ -113,8 +117,7 @@
 
     def body(i, _):
         start = pl.multiple_of(i * size, size)
-        lists = lists_ref[pl.ds(pl.multiple_of(i * chunk, chunk), chunk), :] & (LOW - 1)
-        left = jnp.concatenate([one_hot(sub, lists[m : m + 1, :]) for m in range(chunk)], axis=1)
+        left = jnp.concatenate([one_hot(sub, lists(i * chunk + m) & (LOW - 1)) for m in range(chunk)], axis=1)
         high = high_ref[pl.ds(start, size), :]
         data = data_ref[pl.ds(start, size), :]
         for h in range(0, total_ref.shape[1] // E, 2):
@@ -124,12 +127,12 @@
             total_ref[:, h * E : (h + 2) * E] += jnp.dot(left, right, preferred_element_type=F32)
         return 0
 
-    lax.fori_loop(0, lists_ref.shape[0] // chunk, body, 0)
+    lax.fori_loop(0, data_ref.shape[0] // size, body, 0)
 
 
 def gather_kernel(ids_ref, table_ref, out_ref, spread, wide):
-    ids_t = jnp.transpose(ids_ref[...].astype(F32)).astype(I32)
-    spread_columns(ids_t, CAP, spread)
+    ids = ids_ref[...].reshape(ids_ref.shape[0], 2 * CAP)
+    spread_columns(jnp.transpose(ids.astype(F32)).astype(I32)[:CAP], CAP, spread)
     by_high(table_ref, wide)
     pick_rows(spread, wide, out_ref, 1024)
 
@@ -137,7 +140,7 @@
 def pool_kernel(bag_ref, bag_t_ref, rows_ref, pooled_ref, high, total):
     samples = pooled_ref.shape[0]
     spread_columns((bag_t_ref[...] >> LOW_BITS).astype(F32).astype(BF16), E, high)
-    sum_rows(bag_ref, high, rows_ref, total)
+    sum_rows(lambda k: bag_ref[pl.ds(k, 1), :], high, rows_ref, total)
     for f in range(pooled_ref.shape[1] // E):
         h, low = divmod(f * samples, LOW)
         pooled_ref[:, f * E : (f + 1) * E] = total[low : low + samples, h * E : (h + 1) * E].astype(BF16)
@@ -157,7 +160,7 @@
 
 def head_kernel(
     where_ref, part_ref, pooled_ref, w_near_ref, w_far_ref, labels_ref, w_head_ref,
-    logits_ref, head_ref, grad_ref, *rest
+    logits_ref, head_ref, grad_ref, away_ref, *rest
 ):
     piece_refs, total = rest[:-1], rest[-1]
     pieces, samples, width = grad_ref.shape
@@ -184,8 +187,16 @@
         head_ref[:, cols] = jnp.sum(hidden * dlogit, axis=0, keepdims=True)
         slope = gate * (1.0 + pre * (1.0 - gate))
         grad_ref[q] = (dlogit * w_head_ref[:, cols].astype(F32) * slope).astype(BF16)
-    for e in range(pieces):
-        piece_refs[e][...] = grad_ref[peer(where_ref, e, 1)]
+    for d in range(pieces // 2):
+        piece_refs[d][...] = grad_ref[peer(where_ref, 2 * d, 1)]
+        away_ref[d] = grad_ref[peer(where_ref, 2 * d + 1, 1)]
+
+
+def pack_kernel(near_ref, *refs):
+    for d in range(3):
+        samples = near_ref.shape[1]
+        refs[3 + d][:samples, :] = refs[d][...]
+        refs[3 + d][samples:, :] = near_ref[d + 1]
 
 
 def back_kernel(grad_ref, w_ref, bag_t_ref, out_ref, spread, wide):
@@ -208,9 +219,9 @@
 
 
 def dense_kernel(where_ref, head_ref, *refs):
-    feature_refs, grad_refs, (mine_ref, head_mine_ref, send_ref) = refs[:8], refs[8:16], refs[16:]
+    feature_refs, grad_refs, (mine_ref, head_mine_ref, send_ref) = refs[:8], refs[8:13], refs[13:]
     left = jnp.concatenate([r[...] for r in feature_refs], axis=0)
-    right = jnp.concatenate([r[...] for r in grad_refs], axis=0)
+    right = jnp.concatenate([grad_refs[0][...], grad_refs[1][0]] + [r[...] for r in grad_refs[2:]], axis=0)
     half, width = mine_ref.shape[1:]
     planes = mine_ref.shape[0]
     own = where_ref[3] == 0
@@ -268,16 +279,21 @@
     head_ref[...] = head[0:1] + head[1:2]
 
 
-def scatter_kernel(ids_ref, ids2_ref, data_ref, out_ref, high, total):
-    ids_t = jnp.transpose((ids_ref[...] >> LOW_BITS).astype(F32)).astype(BF16)
-    spread_columns(ids_t, CAP, high)
-    sum_rows(ids2_ref, high, data_ref, total)
+def scatter_kernel(ids_ref, data_ref, out_ref, high, total):
+    ids = ids_ref[...].reshape(ids_ref.shape[0], 2 * CAP)
+    spread_columns(jnp.transpose((ids >> LOW_BITS).astype(F32))[:CAP].astype(BF16), CAP, high)
+    first = lax.broadcasted_iota(I32, (1, E), 1) < CAP
+
+    def lists(k):
+        return jnp.where(first, ids_ref[2 * k], ids_ref[2 * k + 1])
+
+    sum_rows(lists, high, data_ref, total)
     for h in range(out_ref.shape[0] // LOW):
         out_ref[h * LOW : (h + 1) * LOW, :] = total[:, h * E : (h + 1) * E].astype(BF16)
 
 
-def call(kernel, outs, flops, moved, scratch=(), placed=None, mib=16):
-    specs = {}
+def call(kernel, outs, flops, moved, scratch=(), placed=None, mib=16, in_specs=None):
+    specs = {} if in_specs is None else {"in_specs": in_specs}
     if placed is not None:
         specs["in_specs"] = [pl.BlockSpec(memory_space=pltpu.SMEM)] + [pl.BlockSpec(memory_space=pltpu.VMEM)] * placed
     return pl.pallas_call(
@@ -323,17 +339,24 @@
     across = [(g * count + w, (1 - g) * count + t) for g in range(2) for w, t in to_x]
     groups = [[z * 16 + x * 8 + r for z in range(8) for r in range(8)] for x in range(2)]
 
+    small, vmem, far = (pl.BlockSpec(memory_space=m) for m in (pltpu.SMEM, pltpu.VMEM, pltpu.HBM))
     live = jnp.arange(depth, dtype=I32) < lengths[0][:, :, None]
     code = jnp.where(live, owners[0] * (1 << ROWS_BITS) + local_rows[0], -1)
-    code = jnp.transpose(code, (2, 1, 0)).reshape(depth * bags_here, samples)
-    ids, bag, bag_t = call(
+    code = jnp.transpose(code, (1, 2, 0)).reshape(bags_here * depth, samples)
+    ids, bag, bag_t, near_half = pl.pallas_call(
         route_kernel,
-        (shape((count, CAP), I32), shape((count // 2, 2 * CAP), I32), shape((2 * CAP, count // 2), I32)),
-        2 * 4096 * 128 * 1024,
-        100000,
-    )(code)
-    ids, w_early = lax.optimization_barrier((ids, w_first))
-    near_half = lax.dynamic_slice_in_dim(w_early, core * (feats // 2), feats // 2)
+        out_shape=(
+            shape((count, 1, 2 * CAP), I32),
+            shape((count // 2, 2 * CAP), I32),
+            shape((2 * CAP, count // 2), I32),
+            shape((feats // 2, hidden_width), BF16),
+        ),
+        in_specs=[small, vmem, far],
+        out_specs=[vmem] * 4,
+        scratch_shapes=[pltpu.SemaphoreType.DMA],
+        compiler_params=pltpu.CompilerParams(vmem_limit_bytes=58 << 20),
+        cost_estimate=pl.CostEstimate(flops=1 << 30, bytes_accessed=8 << 20, transcendentals=0),
+    )(where, code, w_first)
     near_half = lax.ppermute(near_half, ("grp", "wa"), across)
     far_half = lax.ppermute(near_half, "wa", to_peer[1])
     ids_in = lax.all_to_all(ids, "wa", split_axis=0, concat_axis=0, tiled=True)
@@ -362,14 +385,15 @@
     side_pooled = [lax.ppermute(pooled, "wa", to_peer[2 * d]) for d in range(1, 4)]
 
     width = hidden_width // 8
-    logits, head, grad, *pieces = call(
+    logits, head, grad, away, *pieces = call(
         head_kernel,
         (
             shape((samples, 1), F32),
             shape((1, hidden_width), F32),
             shape((8, samples, width), BF16),
+            shape((4, samples, width), BF16),
         )
-        + (shape((samples, width), BF16),) * 8,
+        + (shape((samples, width), BF16),) * 4,
         2 * samples * feats * hidden_width + samples * hidden_width * 60,
         4 << 20,
         [pltpu.VMEM((samples, hidden_width), F32)],
@@ -390,12 +414,14 @@
         [pltpu.VMEM((slots, E), I32), pltpu.VMEM((LOW, bags // LOW * E), BF16)],
         mib=24,
     )(grad, w_first, bag_t)
-    send, *pieces = lax.optimization_barrier((send, *pieces))
+    near = lax.ppermute(away, "wa", to_peer[1])
+    send, near, *pieces = lax.optimization_barrier((send, near, *pieces))
     arrived = lax.all_to_all(
         send.reshape(count, CAP, E), "wa", split_axis=0, concat_axis=0, tiled=True
     ).reshape(slots, E)
 
-    grads = pieces[:1] + [lax.ppermute(pieces[e], "wa", to_peer[e]) for e in range(1, 8)]
+    packed = call(pack_kernel, (shape((2 * samples, width), BF16),) * 3, 1 << 16, 1 << 20)(near, *pieces[1:])
+    grads = [pieces[0], near] + [lax.ppermute(packed[d - 1], "wa", to_peer[2 * d]) for d in range(1, 4)]
     planes = count // 16
     half = feats // planes // 2
     mine, head_mine, theirs = call(
@@ -407,15 +433,13 @@
         ),
         2 * feats * width * 8 * samples,
         8 << 20,
-        placed=17,
+        placed=14,
     )(where, head, *all_pooled, *grads)
     theirs = lax.ppermute(theirs, "wa", to_x)
     size = half // 8 * (width // E + 1)
     laid = call(cross_kernel, shape((8 * planes * size, E), BF16), 1 << 20, 2 << 20)(mine, head_mine, theirs)
     other_logits = lax.ppermute(logits, "grp", [(0, 1), (1, 0)])
-    laid, ids_pairs, other_logits, arrived = lax.optimization_barrier(
-        (laid, ids_in.reshape(count // 2, 2 * CAP), other_logits, arrived)
-    )
+    laid, other_logits, arrived = lax.optimization_barrier((laid, other_logits, arrived))
     blocks = lax.all_to_all(
         laid.reshape(8 * planes, size, E), "wa", 0, 0, axis_index_groups=groups, tiled=True
     ).reshape(8 * planes * size, E)
@@ -430,7 +454,7 @@
         2 * slots * 4096 * E,
         4 << 20,
         [pltpu.VMEM((slots, E), BF16), pltpu.VMEM((LOW, table.shape[0] // LOW * E), F32)],
-    )(ids_in, ids_pairs, arrived)
+    )(ids_in, arrived)
     logits = jnp.where(group == 0, logits, other_logits)
     return (logits.reshape(samples), dense_grad, head_grad, row_grad)
 

time: 244 us -> 237 us (0.971)
  local copies, waits for them, and re-layouts: 17.3 us -> 12.9 us
  waiting for transfers between devices: 97.4 us -> 94.1 us
    ppermute x7 -> x4, waiting for transfers between devices: 28.2 us -> 20.3 us  [the longest x3 20.3 us: shards(): lax.ppermute(packed[d - 1], 'wa', to_peer[2 * d])]
    dynamic_slice x1 -> x0, local copies, waits for them, and re-layouts: 4.81 us -> none  [shards(): lax.dynamic_slice_in_dim(w_early, core * (feats // 2), feats // 2)]
    ppermute x1, waiting for transfers between devices: 12.8 us -> 17.2 us  [shards(): theirs = lax.ppermute(theirs, 'wa', to_x)]
    all_to_all x1, starting transfers between devices: 13.4 us -> 10.3 us  [shards(): lax.all_to_all(send.reshape(count, CAP, E), 'wa', split_axis=0, concat_ax...]
    pallas_call x1 -> x2, Pallas kernels: 2.44 us -> 5.45 us  [the longest x1 5.39 us: shards(): pl.pallas_call(route_kernel, out_shape=(shape((count, 1, 2 * CAP), I32),...]
    ppermute x7 -> x4, starting transfers between devices: 5.74 us -> 6.67 us  [the longest x3 4.78 us: shards(): lax.ppermute(packed[d - 1], 'wa', to_peer[2 * d])]
    unnamed x50 -> x40, local copies, waits for them, and re-layouts: 10.6 us -> 11 us
  transfers between devices with their start and end apart: 22 -> 19, of which waited for: 10 -> 7; matrix products, arithmetic and copies ran while one was open for 1% -> 0% of each run, Pallas kernels for 17% -> 19%
where the time goes in v1:
time: 237 us; the launch traced here: 236 us
  waiting for transfers between devices  94.1 us (40%)
  Pallas kernels  51.1 us (22%)
  starting transfers between devices  50.6 us (21%)
  blocking collectives  23.9 us (10%)
  local copies, waits for them, and re-layouts  12.9 us (5%)
  other arithmetic  2.64 us (1%)
    ppermute x1, waiting for transfers between devices, shards(): near_half = lax.ppermute(near_half, ('grp', 'wa'), across)  46.7 us
    all_to_all x1, blocking collectives, shards(): ids_in = lax.all_to_all(ids, 'wa', split_axis=0, concat_axis=0, tiled=True)  23.9 us
    ppermute x3, waiting for transfers between devices, shards(): lax.ppermute(packed[d - 1], 'wa', to_peer[2 * d])  20.3 us
    ppermute x1, waiting for transfers between devices, shards(): theirs = lax.ppermute(theirs, 'wa', to_x)  17.2 us
    pallas_call x1, Pallas kernels, shards(): call(scatter_kernel, shape((table.shape[0], E), BF16), 2 * slots * 4096 *...  12.4 us
    all_to_all x1, starting transfers between devices, shards(): lax.all_to_all(laid.reshape(8 * planes, size, E), 'wa', 0, 0, axis_index_...  11.5 us
    pallas_call x1, Pallas kernels, shards(): call(gather_kernel, shape((slots, E), BF16), 2 * slots * 4096 * E, 4 << 2...  11.5 us
    unnamed x40, local copies, waits for them, and re-layouts  11 us
  transfers between devices with their start and end apart: 19, of which 7 were waited for; matrix products, arithmetic and copies ran while one was open for 0% of the time, Pallas kernels for 19%

profile of v1, /device:TPU:1, one launch (start us, length us, event | category | flops | bytes accessed | tf_op | source)
XLA Modules:
  0.0 236.2 jit_solution(6600990439259242432)
XLA Ops:
  2.7 5.4 %shard_map.102 = (s32[128,1,128]{2,1,0:T(1,128)}, s32[64,128]{1,0:T(8,128)}, s32[128,64]{1,0:T(8,128)}, bf16[512,4096]{1,0:T(8,128)(2,1)}) custom-call(s32[5]{0:T(128)} %stack.23.where_ref, s32[32,128]{1,0:T(8,128)} %bitcast.27, bf16[1024,4096]{1,0:T(8,128)(2,1)} %w_ref.5), custom_call_target="tpu_custom_call" | custom-call | flops 1073741824 | bytes 8388608 | tf_op jit(solution)/shard_map/pallas_call | solution.py:346
  8.1 3.4 %collective-permute-start.1 = (bf16[512,4096]{1,0:T(8,128)(2,1)}, bf16[512,4096]{1,0:T(8,128)(2,1)}, u32[]{:S(2)}, u32[]{:S(2)}) collective-permute-start(bf16[512,4096]{1,0:T(8,128)(2,1)} %get-tuple-element.40), channel_id=1, source_target_pairs={{0,136},{1,137},{2,138},{3,139},{4,140},{5,141},{6,142},{7,143},{8... | collective-permute-start | bytes 12582920 | tf_op jit(solution)/shard_map/ppermute | solution.py:360
  11.5 23.9 %all_to_all.20.ids_ref = s32[128,1,128]{2,1,0:T(1,128)S(1)} all-to-all(s32[128,1,128]{2,1,0:T(1,128)} %get-tuple-element.39), channel_id=1, replica_groups=mesh['grp'=2,'wa'=128] {'wa'}, dimensions={0} | all-to-all | bytes 131072 | tf_op jit(solution)/shard_map/all_to_all | solution.py:362
  35.4 11.5 %shard_map.103 = bf16[8192,128]{1,0:T(8,128)(2,1)S(1)} custom-call(s32[128,1,128]{2,1,0:T(1,128)S(1)} %all_to_all.20.ids_ref, bf16[4096,128]{1,0:T(8,128)(2,1)S(1)} %copy-done.4), custom_call_target="tpu_custom_call" | custom-call | flops 8589934592 | bytes 4194304 | tf_op jit(solution)/shard_map/pallas_call | solution.py:363
  48.3 6.0 %all-to-all-start.1 = ((bf16[128,64,128]{2,1,0:T(8,128)(2,1)}), bf16[128,64,128]{2,1,0:T(8,128)(2,1)S(1)}, u32[]{:S(2)}, u32[]{:S(2)}) async-start(bf16[128,64,128]{2,1,0:T(8,128)(2,1)} %bitcast.26), calls=%async_computation.1 | async-start | bytes 4194304 | tf_op jit(solution)/shard_map/all_to_all | solution.py:370
  54.3 46.7 %collective-permute-done.1.w_near_ref = bf16[512,4096]{1,0:T(8,128)(2,1)} collective-permute-done((bf16[512,4096]{1,0:T(8,128)(2,1)}, bf16[512,4096]{1,0:T(8,128)(2,1)}, u32[]{:S(2)}, u32[]{:S(2)}) %collective-permute-start.1) | collective-permute-done | bytes 4194336 | tf_op jit(solution)/shard_map/ppermute | solution.py:360
  101.1 2.3 collective-permute-start.2
  103.4 2.5 %all-to-all-done.1 = bf16[128,64,128]{2,1,0:T(8,128)(2,1)S(1)} async-done(((bf16[128,64,128]{2,1,0:T(8,128)(2,1)}), bf16[128,64,128]{2,1,0:T(8,128)(2,1)S(1)}, u32[]{:S(2)}, u32[]{:S(2)}) %all-to-all-start.1) | async-done | bytes 2097184 | tf_op jit(solution)/shard_map/all_to_all | solution.py:370
  105.8 4.5 %shard_map.104.pooled_ref.refs_0_ = bf16[128,1024]{1,0:T(8,128)(2,1)S(1)} custom-call(s32[64,128]{1,0:T(8,128)S(1)} %copy-done.13, s32[128,64]{1,0:T(8,128)S(1)} %copy-done.11, bf16[8192,128]{1,0:T(8,128)(2,1)S(1)} %bitcast.25), custom_call_target="tpu_custom_call" | custom-call | flops 2147483648 | bytes 4194304 | tf_op jit(solution)/shard_map/pallas_call | solution.py:373
  112.1 2.7 %collective-permute-start.5 = (bf16[128,1024]{1,0:T(8,128)(2,1)S(1)}, bf16[128,1024]{1,0:T(8,128)(2,1)S(1)}, u32[]{:S(2)}, u32[]{:S(2)}) collective-permute-start(bf16[128,1024]{1,0:T(8,128)(2,1)S(1)} %shard_map.104.pooled_ref.refs_0_), channel_id=1, source_target_pairs={{0,4},{1,5},{2,6},{3,7},{4,0},{5,1},{6,2},{7,3},{8,12},{9,13},{10,... | collective-permute-start | bytes 786440 | tf_op jit(solution)/shard_map/ppermute | solution.py:385
  115.8 3.4 %copy-done = bf16[1024,4096]{1,0:T(8,128)(2,1)S(1)} copy-done((bf16[1024,4096]{1,0:T(8,128)(2,1)S(1)}, bf16[1024,4096]{1,0:T(8,128)(2,1)}, u32[]{:S(2)}) %copy-start) | copy-done | bytes 8388632
  120.5 6.0 %shard_map.106 = (f32[128,1]{1,0:T(8,128)S(1)}, f32[1,4096]{1,0:T(1,128)S(1)}, bf16[8,128,512]{2,1,0:T(8,128)(2,1)S(1)}, bf16[4,128,512]{2,1,0:T(8,128)(2,1)S(1)...) custom-call(s32[5]{0:T(128)S(1)} %copy-done.3, ...), custom_call_target="tpu_custom_call" | custom-call | flops 1105199104 | bytes 4194304 | tf_op jit(solution)/shard_map/pallas_call | solution.py:388
  127.1 1.9 collective-permute-start.10
  129.7 6.4 %shard_map.107 = bf16[8192,128]{1,0:T(8,128)(2,1)S(1)} custom-call(bf16[8,128,512]{2,1,0:T(8,128)(2,1)S(1)} %get-tuple-element.47.grad_ref, bf16[1024,4096]{1,0:T(8,128)(2,1)S(1)} %bitcast.21, s32[128,64]{1,0:T(8,128)S(1)} %copy-done.12), custom_call_target="tpu_custom_call" | custom-call | flops 3221225472 | bytes 12582912 | tf_op jit(solution)/shard_map/pallas_call | solution.py:409
  137.5 10.3 %all-to-all-start.2 = ((bf16[128,64,128]{2,1,0:T(8,128)(2,1)}), bf16[128,64,128]{2,1,0:T(8,128)(2,1)S(1)}, u32[]{:S(2)}, u32[]{:S(2)}) async-start(bf16[128,64,128]{2,1,0:T(8,128)(2,1)} %bitcast.24), calls=%async_computation.2 | async-start | bytes 4194304 | tf_op jit(solution)/shard_map/all_to_all | solution.py:419
  150.6 2.4 %collective-permute-start.12 = (bf16[256,512]{1,0:T(8,128)(2,1)S(1)}, bf16[256,512]{1,0:T(8,128)(2,1)S(1)}, u32[]{:S(2)}, u32[]{:S(2)}) collective-permute-start(bf16[256,512]{1,0:T(8,128)(2,1)S(1)} %get-tuple-element.59), channel_id=1, source_target_pairs={{0,4},{1,5},{2,6},{3,7},{4,0},{5,1},{6,2},{7,3},{8,12},{9,13},{10,... | collective-permute-start | bytes 786440 | tf_op jit(solution)/shard_map/ppermute | solution.py:424
  154.2 9.3 %collective-permute-done.11.refs_10_ = bf16[256,512]{1,0:T(8,128)(2,1)S(1)} collective-permute-done((bf16[256,512]{1,0:T(8,128)(2,1)S(1)}, bf16[256,512]{1,0:T(8,128)(2,1)S(1)}, u32[]{:S(2)}, u32[]{:S(2)}) %collective-permute-start.11) | collective-permute-done | bytes 262176 | tf_op jit(solution)/shard_map/ppermute | solution.py:424
  163.5 11.0 %collective-permute-done.12.refs_11_ = bf16[256,512]{1,0:T(8,128)(2,1)S(1)} collective-permute-done((bf16[256,512]{1,0:T(8,128)(2,1)S(1)}, bf16[256,512]{1,0:T(8,128)(2,1)S(1)}, u32[]{:S(2)}, u32[]{:S(2)}) %collective-permute-start.12) | collective-permute-done | bytes 262176 | tf_op jit(solution)/shard_map/ppermute | solution.py:424
  178.1 1.9 shard_map.109
  179.9 2.0 collective-permute-start.14
  183.5 17.2 %collective-permute-done.14.theirs_ref = bf16[528,512]{1,0:T(8,128)(2,1)S(1)} collective-permute-done((bf16[528,512]{1,0:T(8,128)(2,1)S(1)}, bf16[528,512]{1,0:T(8,128)(2,1)S(1)}, u32[]{:S(2)}, u32[]{:S(2)}) %collective-permute-start.14) | collective-permute-done | bytes 540704 | tf_op jit(solution)/shard_map/ppermute | solution.py:438
  201.8 11.5 %all-to-all-start.3 = ((bf16[64,40,128]{2,1,0:T(8,128)(2,1)}), bf16[64,40,128]{2,1,0:T(8,128)(2,1)S(1)}, u32[]{:S(2)}, u32[]{:S(2)}) async-start(bf16[64,40,128]{2,1,0:T(8,128)(2,1)} %bitcast.14), calls=%async_computation.3 | async-start | bytes 1310720 | tf_op jit(solution)/shard_map/all_to_all | solution.py:443
  214.0 12.4 %shard_map.112 = bf16[4096,128]{1,0:T(8,128)(2,1)} custom-call(s32[128,1,128]{2,1,0:T(1,128)S(1)} %all_to_all.20.ids_ref, bf16[8192,128]{1,0:T(8,128)(2,1)S(1)} %bitcast.23), custom_call_target="tpu_custom_call" | custom-call | flops 8589934592 | bytes 4194304 | tf_op jit(solution)/shard_map/pallas_call | solution.py:451
  226.4 7.3 %all-to-all-done.3 = bf16[64,40,128]{2,1,0:T(8,128)(2,1)S(1)} async-done(((bf16[64,40,128]{2,1,0:T(8,128)(2,1)}), bf16[64,40,128]{2,1,0:T(8,128)(2,1)S(1)}, u32[]{:S(2)}, u32[]{:S(2)}) %all-to-all-start.3) | async-done | bytes 655392 | tf_op jit(solution)/shard_map/all_to_all | solution.py:443
  (76 shorter events, 23.4 us)
Async XLA Ops:
  2.7 32.7 %copy-start.4 = (bf16[4096,128]{1,0:T(8,128)(2,1)S(1)}, bf16[4096,128]{1,0:T(8,128)(2,1)}, u32[]{:S(2)}) copy-start(bf16[4096,128]{1,0:T(8,128)(2,1)} %table_ref.1) | copy-start | bytes 3145732
  8.1 93.0 %collective-permute-start.1 = (bf16[512,4096]{1,0:T(8,128)(2,1)}, bf16[512,4096]{1,0:T(8,128)(2,1)}, u32[]{:S(2)}, u32[]{:S(2)}) collective-permute-start(bf16[512,4096]{1,0:T(8,128)(2,1)} %get-tuple-element.40), channel_id=1, source_target_pairs={{0,136},{1,137},{2,138},{3,139},{4,140},{5,141},{6,142},{7,143},{8... | collective-permute-start | bytes 12582920 | tf_op jit(solution)/shard_map/ppermute | solution.py:360
  48.3 57.5 %copy-start.11 = (s32[128,64]{1,0:T(8,128)S(1)}, s32[128,64]{1,0:T(8,128)}, u32[]{:S(2)}) copy-start(s32[128,64]{1,0:T(8,128)} %get-tuple-element.38.bag_t_ref) | copy-start | bytes 98308
  48.3 57.5 %copy-start.13 = (s32[64,128]{1,0:T(8,128)S(1)}, s32[64,128]{1,0:T(8,128)}, u32[]{:S(2)}) copy-start(s32[64,128]{1,0:T(8,128)} %get-tuple-element.37.bag_ref) | copy-start | bytes 98308
  48.3 57.5 %all-to-all-start.1 = ((bf16[128,64,128]{2,1,0:T(8,128)(2,1)}), bf16[128,64,128]{2,1,0:T(8,128)(2,1)S(1)}, u32[]{:S(2)}, u32[]{:S(2)}) async-start(bf16[128,64,128]{2,1,0:T(8,128)(2,1)} %bitcast.26), calls=%async_computation.1 | async-start | bytes 4194304 | tf_op jit(solution)/shard_map/all_to_all | solution.py:370
  101.1 19.4 %collective-permute-start.2 = (bf16[512,4096]{1,0:T(8,128)(2,1)}, bf16[512,4096]{1,0:T(8,128)(2,1)}, u32[]{:S(2)}, u32[]{:S(2)}) collective-permute-start(bf16[512,4096]{1,0:T(8,128)(2,1)} %collective-permute-done.1.w_near_ref), channel_id=1, source_target_pairs={{0,1},{1,0},{2,3},{3,2},{4,5},{5,4},{6,7},{7,6},{8,9},{9,8},{10,11... | collective-permute-start | bytes 12582920 | tf_op jit(solution)/shard_map/ppermute | solution.py:361
  110.3 10.1 %collective-permute-start = (bf16[128,1024]{1,0:T(8,128)(2,1)S(1)}, bf16[128,1024]{1,0:T(8,128)(2,1)S(1)}, u32[]{:S(2)}, u32[]{:S(2)}) collective-permute-start(bf16[128,1024]{1,0:T(8,128)(2,1)S(1)} %shard_map.104.pooled_ref.refs_0_), channel_id=1, source_target_pairs={{0,128},{128,0},{1,129},{129,1},{2,130},{130,2},{3,131},{131,3},{4... | collective-permute-start | bytes 786440 | tf_op jit(solution)/shard_map/ppermute | solution.py:380
  111.7 17.3 %collective-permute-start.4 = (bf16[128,1024]{1,0:T(8,128)(2,1)S(1)}, bf16[128,1024]{1,0:T(8,128)(2,1)S(1)}, u32[]{:S(2)}, u32[]{:S(2)}) collective-permute-start(bf16[128,1024]{1,0:T(8,128)(2,1)S(1)} %shard_map.104.pooled_ref.refs_0_), channel_id=1, source_target_pairs={{0,2},{1,3},{2,4},{3,5},{4,6},{5,7},{6,0},{7,1},{8,10},{9,11},{10,... | collective-permute-start | bytes 786440 | tf_op jit(solution)/shard_map/ppermute | solution.py:385
  112.1 16.9 %collective-permute-start.5 = (bf16[128,1024]{1,0:T(8,128)(2,1)S(1)}, bf16[128,1024]{1,0:T(8,128)(2,1)S(1)}, u32[]{:S(2)}, u32[]{:S(2)}) collective-permute-start(bf16[128,1024]{1,0:T(8,128)(2,1)S(1)} %shard_map.104.pooled_ref.refs_0_), channel_id=1, source_target_pairs={{0,4},{1,5},{2,6},{3,7},{4,0},{5,1},{6,2},{7,3},{8,12},{9,13},{10,... | collective-permute-start | bytes 786440 | tf_op jit(solution)/shard_map/ppermute | solution.py:385
  114.8 14.2 %collective-permute-start.6 = (bf16[128,1024]{1,0:T(8,128)(2,1)S(1)}, bf16[128,1024]{1,0:T(8,128)(2,1)S(1)}, u32[]{:S(2)}, u32[]{:S(2)}) collective-permute-start(bf16[128,1024]{1,0:T(8,128)(2,1)S(1)} %shard_map.104.pooled_ref.refs_0_), channel_id=1, source_target_pairs={{0,6},{1,7},{2,0},{3,1},{4,2},{5,3},{6,4},{7,5},{8,14},{9,15},{10,... | collective-permute-start | bytes 786440 | tf_op jit(solution)/shard_map/ppermute | solution.py:385
  119.1 10.6 %slice-start = ((s8[8388608]{0:T(1024)(128)(4,1)}), s8[4194304]{0:T(1024)(128)(4,1)S(1)}, s32[]{:S(2)}) async-start(s8[8388608]{0:T(1024)(128)(4,1)} %bitcast.20), calls=%async_computation.4 | async-start | bytes 8388608
  120.4 9.3 %slice-start.1 = ((s8[8388608]{0:T(1024)(128)(4,1)}), s8[4194304]{0:T(1024)(128)(4,1)S(1)}, s32[]{:S(2)}) async-start(s8[8388608]{0:T(1024)(128)(4,1)} %bitcast.20), calls=%async_computation.5 | async-start | bytes 8388608
  127.1 10.4 %collective-permute-start.10 = (bf16[4,128,512]{2,1,0:T(8,128)(2,1)S(1)}, bf16[4,128,512]{2,1,0:T(8,128)(2,1)S(1)}, u32[]{:S(2)}, u32[]{:S(2)}) collective-permute-start(bf16[4,128,512]{2,1,0:T(8,128)(2,1)S(1)} %get-tuple-element.48), channel_id=1, source_target_pairs={{0,1},{1,0},{2,3},{3,2},{4,5},{5,4},{6,7},{7,6},{8,9},{9,8},{10,11... | collective-permute-start | bytes 1572872 | tf_op jit(solution)/shard_map/ppermute | solution.py:417
  137.5 64.2 %all-to-all-start.2 = ((bf16[128,64,128]{2,1,0:T(8,128)(2,1)}), bf16[128,64,128]{2,1,0:T(8,128)(2,1)S(1)}, u32[]{:S(2)}, u32[]{:S(2)}) async-start(bf16[128,64,128]{2,1,0:T(8,128)(2,1)} %bitcast.24), calls=%async_computation.2 | async-start | bytes 4194304 | tf_op jit(solution)/shard_map/all_to_all | solution.py:419
  147.8 2.9 %collective-permute-start.3 = (bf16[128,1024]{1,0:T(8,128)(2,1)S(1)}, bf16[128,1024]{1,0:T(8,128)(2,1)S(1)}, u32[]{:S(2)}, u32[]{:S(2)}) collective-permute-start(bf16[128,1024]{1,0:T(8,128)(2,1)S(1)} %shard_map.104.pooled_ref.refs_0_), channel_id=1, source_target_pairs={{0,1},{1,0},{2,3},{3,2},{4,5},{5,4},{6,7},{7,6},{8,9},{9,8},{10,11... | collective-permute-start | bytes 786440 | tf_op jit(solution)/shard_map/ppermute | solution.py:407
  148.8 4.3 %collective-permute-start.7 = (bf16[128,1024]{1,0:T(8,128)(2,1)}, bf16[128,1024]{1,0:T(8,128)(2,1)S(1)}, u32[]{:S(2)}, u32[]{:S(2)}) collective-permute-start(bf16[128,1024]{1,0:T(8,128)(2,1)} %copy-done.5), channel_id=1, source_target_pairs={{0,1},{1,0},{2,3},{3,2},{4,5},{5,4},{6,7},{7,6},{8,9},{9,8},{10,11... | collective-permute-start | bytes 786440 | tf_op jit(solution)/shard_map/ppermute | solution.py:407
  148.9 5.4 %collective-permute-start.8 = (bf16[128,1024]{1,0:T(8,128)(2,1)}, bf16[128,1024]{1,0:T(8,128)(2,1)S(1)}, u32[]{:S(2)}, u32[]{:S(2)}) collective-permute-start(bf16[128,1024]{1,0:T(8,128)(2,1)} %copy-done.7), channel_id=1, source_target_pairs={{0,1},{1,0},{2,3},{3,2},{4,5},{5,4},{6,7},{7,6},{8,9},{9,8},{10,11... | collective-permute-start | bytes 786440 | tf_op jit(solution)/shard_map/ppermute | solution.py:407
  149.3 4.9 %collective-permute-start.9 = (bf16[128,1024]{1,0:T(8,128)(2,1)}, bf16[128,1024]{1,0:T(8,128)(2,1)S(1)}, u32[]{:S(2)}, u32[]{:S(2)}) collective-permute-start(bf16[128,1024]{1,0:T(8,128)(2,1)} %copy-done.9), channel_id=1, source_target_pairs={{0,1},{1,0},{2,3},{3,2},{4,5},{5,4},{6,7},{7,6},{8,9},{9,8},{10,11... | collective-permute-start | bytes 786440 | tf_op jit(solution)/shard_map/ppermute | solution.py:407
  149.4 14.1 %collective-permute-start.11 = (bf16[256,512]{1,0:T(8,128)(2,1)S(1)}, bf16[256,512]{1,0:T(8,128)(2,1)S(1)}, u32[]{:S(2)}, u32[]{:S(2)}) collective-permute-start(bf16[256,512]{1,0:T(8,128)(2,1)S(1)} %get-tuple-element.58), channel_id=1, source_target_pairs={{0,2},{1,3},{2,4},{3,5},{4,6},{5,7},{6,0},{7,1},{8,10},{9,11},{10,... | collective-permute-start | bytes 786440 | tf_op jit(solution)/shard_map/ppermute | solution.py:424
  150.6 23.9 %collective-permute-start.12 = (bf16[256,512]{1,0:T(8,128)(2,1)S(1)}, bf16[256,512]{1,0:T(8,128)(2,1)S(1)}, u32[]{:S(2)}, u32[]{:S(2)}) collective-permute-start(bf16[256,512]{1,0:T(8,128)(2,1)S(1)} %get-tuple-element.59), channel_id=1, source_target_pairs={{0,4},{1,5},{2,6},{3,7},{4,0},{5,1},{6,2},{7,3},{8,12},{9,13},{10,... | collective-permute-start | bytes 786440 | tf_op jit(solution)/shard_map/ppermute | solution.py:424
  153.0 21.5 %collective-permute-start.13 = (bf16[256,512]{1,0:T(8,128)(2,1)S(1)}, bf16[256,512]{1,0:T(8,128)(2,1)S(1)}, u32[]{:S(2)}, u32[]{:S(2)}) collective-permute-start(bf16[256,512]{1,0:T(8,128)(2,1)S(1)} %get-tuple-element.60), channel_id=1, source_target_pairs={{0,6},{1,7},{2,0},{3,1},{4,2},{5,3},{6,4},{7,5},{8,14},{9,15},{10,... | collective-permute-start | bytes 786440 | tf_op jit(solution)/shard_map/ppermute | solution.py:424
  179.9 20.7 %collective-permute-start.14 = (bf16[528,512]{1,0:T(8,128)(2,1)S(1)}, bf16[528,512]{1,0:T(8,128)(2,1)S(1)}, u32[]{:S(2)}, u32[]{:S(2)}) collective-permute-start(bf16[528,512]{1,0:T(8,128)(2,1)S(1)} %get-tuple-element.63), channel_id=1, source_target_pairs={{0,8},{1,9},{2,10},{3,11},{4,12},{5,13},{6,14},{7,15},{8,0},{9,1},... | collective-permute-start | bytes 1622024 | tf_op jit(solution)/shard_map/ppermute | solution.py:438
  181.9 19.8 %collective-permute-start.15 = (f32[128,1]{1,0:T(8,128)S(1)}, f32[128,1]{1,0:T(8,128)S(1)}, u32[]{:S(2)}, u32[]{:S(2)}) collective-permute-start(f32[128,1]{1,0:T(8,128)S(1)} %get-tuple-element.41), channel_id=1, source_target_pairs={{0,128},{128,0},{1,129},{129,1},{2,130},{130,2},{3,131},{131,3},{4... | collective-permute-start | bytes 1544 | tf_op jit(solution)/shard_map/ppermute | solution.py:441
  201.8 31.9 %all-to-all-start.3 = ((bf16[64,40,128]{2,1,0:T(8,128)(2,1)}), bf16[64,40,128]{2,1,0:T(8,128)(2,1)S(1)}, u32[]{:S(2)}, u32[]{:S(2)}) async-start(bf16[64,40,128]{2,1,0:T(8,128)(2,1)} %bitcast.14), calls=%async_computation.3 | async-start | bytes 1310720 | tf_op jit(solution)/shard_map/all_to_all | solution.py:443
  (15 other events, 54.1 us)

commit v2 on v1

--- a/solution.py
+++ b/solution.py
@@ -22,9 +22,10 @@
     return jnp.where(left == right, 1.0, 0.0).astype(BF16)
 
 
-def route_kernel(where_ref, code_ref, w_ref, ids_ref, bag_ref, bag_t_ref, half_ref, sem):
+def route_kernel(code_ref, w_ref, ids_ref, bag_ref, bag_t_ref, half_ref, sem):
     rows = half_ref.shape[0]
-    copy = pltpu.make_async_copy(w_ref.at[pl.ds(pl.multiple_of(where_ref[2] * rows, rows), rows), :], half_ref, sem)
+    start = pl.multiple_of(lax.axis_index("wa") % 2 * rows, rows)
+    copy = pltpu.make_async_copy(w_ref.at[pl.ds(start, rows), :], half_ref, sem)
     copy.start()
     lines = code_ref.shape[0]
     owners = ids_ref.shape[0]
@@ -106,7 +107,7 @@
         out_ref[pl.ds(start, block), :] = total.astype(BF16)
         return 0
 
-    lax.fori_loop(0, out_ref.shape[0] // block, body, 0)
+    lax.fori_loop(0, out_ref.shape[0] // block, body, 0, unroll=True)
 
 
 def sum_rows(lists, high_ref, data_ref, total_ref):
@@ -127,7 +128,7 @@
             total_ref[:, h * E : (h + 2) * E] += jnp.dot(left, right, preferred_element_type=F32)
         return 0
 
-    lax.fori_loop(0, data_ref.shape[0] // size, body, 0)
+    lax.fori_loop(0, data_ref.shape[0] // size, body, 0, unroll=4)
 
 
 def gather_kernel(ids_ref, table_ref, out_ref, spread, wide):
@@ -218,9 +219,14 @@
     pick_rows(spread, wide, out_ref, 1024)
 
 
+def stack_kernel(*refs):
+    for e, ref in enumerate(refs[:-1]):
+        rows = ref.shape[0]
+        refs[-1][e * rows : (e + 1) * rows, :] = ref[...]
+
+
 def dense_kernel(where_ref, head_ref, *refs):
-    feature_refs, grad_refs, (mine_ref, head_mine_ref, send_ref) = refs[:8], refs[8:13], refs[13:]
-    left = jnp.concatenate([r[...] for r in feature_refs], axis=0)
+    left_ref, grad_refs, (mine_ref, head_mine_ref, send_ref) = refs[0], refs[1:6], refs[6:]
     right = jnp.concatenate([grad_refs[0][...], grad_refs[1][0]] + [r[...] for r in grad_refs[2:]], axis=0)
     half, width = mine_ref.shape[1:]
     planes = mine_ref.shape[0]
@@ -236,7 +242,7 @@
     send_ref[planes * half :, :] = jnp.concatenate([tail] * (width // E), axis=1)
     for z in range(planes):
         both = lax.dot_general(
-            left[:, 2 * half * z : 2 * half * (z + 1)], right, (((0,), (0,)), ((), ())), preferred_element_type=F32
+            left_ref[:, 2 * half * z : 2 * half * (z + 1)], right, (((0,), (0,)), ((), ())), preferred_element_type=F32
         )
         mine_ref[z] = jnp.where(own, both[:half], both[half:])
         send_ref[z * half : (z + 1) * half, :] = jnp.where(own, both[half:], both[:half]).astype(BF16)
@@ -351,12 +357,12 @@
             shape((2 * CAP, count // 2), I32),
             shape((feats // 2, hidden_width), BF16),
         ),
-        in_specs=[small, vmem, far],
+        in_specs=[vmem, far],
         out_specs=[vmem] * 4,
         scratch_shapes=[pltpu.SemaphoreType.DMA],
         compiler_params=pltpu.CompilerParams(vmem_limit_bytes=58 << 20),
         cost_estimate=pl.CostEstimate(flops=1 << 30, bytes_accessed=8 << 20, transcendentals=0),
-    )(where, code, w_first)
+    )(code, w_first)
     near_half = lax.ppermute(near_half, ("grp", "wa"), across)
     far_half = lax.ppermute(near_half, "wa", to_peer[1])
     ids_in = lax.all_to_all(ids, "wa", split_axis=0, concat_axis=0, tiled=True)
@@ -422,6 +428,7 @@
 
     packed = call(pack_kernel, (shape((2 * samples, width), BF16),) * 3, 1 << 16, 1 << 20)(near, *pieces[1:])
     grads = [pieces[0], near] + [lax.ppermute(packed[d - 1], "wa", to_peer[2 * d]) for d in range(1, 4)]
+    left = call(stack_kernel, shape((8 * samples, feats), BF16), 1 << 16, 4 << 20)(*all_pooled)
     planes = count // 16
     half = feats // planes // 2
     mine, head_mine, theirs = call(
@@ -433,8 +440,8 @@
         ),
         2 * feats * width * 8 * samples,
         8 << 20,
-        placed=14,
-    )(where, head, *all_pooled, *grads)
+        placed=7,
+    )(where, head, left, *grads)
     theirs = lax.ppermute(theirs, "wa", to_x)
     size = half // 8 * (width // E + 1)
     laid = call(cross_kernel, shape((8 * planes * size, E), BF16), 1 << 20, 2 << 20)(mine, head_mine, theirs)

time: 237 us -> 236 us (level); the launches traced: 236 us -> 231 us
  Pallas kernels: 51.1 us -> 45.8 us
  local copies, waits for them, and re-layouts: 12.9 us -> 10.2 us
    pallas_call x1, Pallas kernels: 11.5 us -> 9.14 us  [shards(): call(gather_kernel, shape((slots, E), BF16), 2 * slots * 4096 * E, 4 << 2...]
    unnamed x40 -> x50, local copies, waits for them, and re-layouts: 11 us -> 8.86 us
  transfers between devices with their start and end apart: 19 -> 19, of which waited for: 7 -> 7; matrix products, arithmetic and copies ran while one was open for 0% -> 0% of each run, Pallas kernels for 19% -> 17%
where the time goes in v2:
time: 236 us; the launch traced here: 231 us
  waiting for transfers between devices  95.7 us (41%)
  starting transfers between devices  51.7 us (22%)
  Pallas kernels  45.8 us (19%)
  blocking collectives  24.2 us (10%)
  local copies, waits for them, and re-layouts  10.2 us (4%)
  other arithmetic  2.63 us (1%)
    ppermute x1, waiting for transfers between devices, shards(): near_half = lax.ppermute(near_half, ('grp', 'wa'), across)  48.9 us
    all_to_all x1, blocking collectives, shards(): ids_in = lax.all_to_all(ids, 'wa', split_axis=0, concat_axis=0, tiled=True)  24.2 us
    ppermute x1, waiting for transfers between devices, shards(): theirs = lax.ppermute(theirs, 'wa', to_x)  19.2 us
    ppermute x3, waiting for transfers between devices, shards(): lax.ppermute(packed[d - 1], 'wa', to_peer[2 * d])  19 us
    all_to_all x1, starting transfers between devices, shards(): lax.all_to_all(send.reshape(count, CAP, E), 'wa', split_axis=0, concat_ax...  12.4 us
    pallas_call x1, Pallas kernels, shards(): call(scatter_kernel, shape((table.shape[0], E), BF16), 2 * slots * 4096 *...  11.2 us
    all_to_all x1, starting transfers between devices, shards(): lax.all_to_all(laid.reshape(8 * planes, size, E), 'wa', 0, 0, axis_index_...  10.8 us
    pallas_call x1, Pallas kernels, shards(): call(gather_kernel, shape((slots, E), BF16), 2 * slots * 4096 * E, 4 << 2...  9.14 us
  transfers between devices with their start and end apart: 19, of which 7 were waited for; matrix products, arithmetic and copies ran while one was open for 0% of the time, Pallas kernels for 17%

profile of v2, /device:TPU:1, one launch (start us, length us, event | category | flops | bytes accessed | tf_op | source)
XLA Modules:
  0.0 231.5 jit_solution(10516414428691073273)
XLA Ops:
  2.0 5.4 %shard_map.102 = (s32[128,1,128]{2,1,0:T(1,128)}, s32[64,128]{1,0:T(8,128)}, s32[128,64]{1,0:T(8,128)}, bf16[512,4096]{1,0:T(8,128)(2,1)}) custom-call(s32[32,128]{1,0:T(8,128)} %bitcast.27, bf16[1024,4096]{1,0:T(8,128)(2,1)} %w_ref.5), custom_call_target="tpu_custom_call" | custom-call | flops 1073741824 | bytes 8388608 | tf_op jit(solution)/shard_map/pallas_call | solution.py:352
  7.4 3.4 %collective-permute-start.1 = (bf16[512,4096]{1,0:T(8,128)(2,1)}, bf16[512,4096]{1,0:T(8,128)(2,1)}, u32[]{:S(2)}, u32[]{:S(2)}) collective-permute-start(bf16[512,4096]{1,0:T(8,128)(2,1)} %get-tuple-element.40), channel_id=1, source_target_pairs={{0,136},{1,137},{2,138},{3,139},{4,140},{5,141},{6,142},{7,143},{8... | collective-permute-start | bytes 12582920 | tf_op jit(solution)/shard_map/ppermute | solution.py:366
  10.8 24.2 %all_to_all.20.ids_ref = s32[128,1,128]{2,1,0:T(1,128)S(1)} all-to-all(s32[128,1,128]{2,1,0:T(1,128)} %get-tuple-element.39), channel_id=1, replica_groups=mesh['grp'=2,'wa'=128] {'wa'}, dimensions={0} | all-to-all | bytes 131072 | tf_op jit(solution)/shard_map/all_to_all | solution.py:368
  34.9 9.1 %shard_map.103 = bf16[8192,128]{1,0:T(8,128)(2,1)S(1)} custom-call(s32[128,1,128]{2,1,0:T(1,128)S(1)} %all_to_all.20.ids_ref, bf16[4096,128]{1,0:T(8,128)(2,1)S(1)} %copy-done.13), custom_call_target="tpu_custom_call" | custom-call | flops 8589934592 | bytes 4194304 | tf_op jit(solution)/shard_map/pallas_call | solution.py:369
  45.4 6.0 %all-to-all-start.1 = ((bf16[128,64,128]{2,1,0:T(8,128)(2,1)}), bf16[128,64,128]{2,1,0:T(8,128)(2,1)S(1)}, u32[]{:S(2)}, u32[]{:S(2)}) async-start(bf16[128,64,128]{2,1,0:T(8,128)(2,1)} %bitcast.26), calls=%async_computation.1 | async-start | bytes 4194304 | tf_op jit(solution)/shard_map/all_to_all | solution.py:376
  51.4 48.9 %collective-permute-done.1.w_near_ref = bf16[512,4096]{1,0:T(8,128)(2,1)} collective-permute-done((bf16[512,4096]{1,0:T(8,128)(2,1)}, bf16[512,4096]{1,0:T(8,128)(2,1)}, u32[]{:S(2)}, u32[]{:S(2)}) %collective-permute-start.1) | collective-permute-done | bytes 4194336 | tf_op jit(solution)/shard_map/ppermute | solution.py:366
  100.3 2.5 %collective-permute-start.2 = (bf16[512,4096]{1,0:T(8,128)(2,1)}, bf16[512,4096]{1,0:T(8,128)(2,1)}, u32[]{:S(2)}, u32[]{:S(2)}) collective-permute-start(bf16[512,4096]{1,0:T(8,128)(2,1)} %collective-permute-done.1.w_near_ref), channel_id=1, source_target_pairs={{0,1},{1,0},{2,3},{3,2},{4,5},{5,4},{6,7},{7,6},{8,9},{9,8},{10,11... | collective-permute-start | bytes 12582920 | tf_op jit(solution)/shard_map/ppermute | solution.py:367
  102.9 3.7 %shard_map.104.pooled_ref.refs_0_ = bf16[128,1024]{1,0:T(8,128)(2,1)S(1)} custom-call(s32[64,128]{1,0:T(8,128)S(1)} %copy-done.18, s32[128,64]{1,0:T(8,128)S(1)} %copy-done.16, bf16[8192,128]{1,0:T(8,128)(2,1)S(1)} %bitcast.25), custom_call_target="tpu_custom_call" | custom-call | flops 2147483648 | bytes 4194304 | tf_op jit(solution)/shard_map/pallas_call | solution.py:379
  106.6 1.7 collective-permute-start
  109.9 2.6 %collective-permute-start.5 = (bf16[128,1024]{1,0:T(8,128)(2,1)S(1)}, bf16[128,1024]{1,0:T(8,128)(2,1)S(1)}, u32[]{:S(2)}, u32[]{:S(2)}) collective-permute-start(bf16[128,1024]{1,0:T(8,128)(2,1)S(1)} %shard_map.104.pooled_ref.refs_0_), channel_id=1, source_target_pairs={{0,4},{1,5},{2,6},{3,7},{4,0},{5,1},{6,2},{7,3},{8,12},{9,13},{10,... | collective-permute-start | bytes 786440 | tf_op jit(solution)/shard_map/ppermute | solution.py:391
  113.6 3.4 %copy-done = bf16[1024,4096]{1,0:T(8,128)(2,1)S(1)} copy-done((bf16[1024,4096]{1,0:T(8,128)(2,1)S(1)}, bf16[1024,4096]{1,0:T(8,128)(2,1)}, u32[]{:S(2)}) %copy-start) | copy-done | bytes 8388632
  118.3 6.0 %shard_map.106 = (f32[128,1]{1,0:T(8,128)S(1)}, f32[1,4096]{1,0:T(1,128)S(1)}, bf16[8,128,512]{2,1,0:T(8,128)(2,1)S(1)}, bf16[4,128,512]{2,1,0:T(8,128)(2,1)S(1)...) custom-call(s32[5]{0:T(128)S(1)} %stack.23.where_ref, ...), custom_call_target="tpu_custom_call" | custom-call | flops 1105199104 | bytes 4194304 | tf_op jit(solution)/shard_map/pallas_call | solution.py:394
  124.4 1.6 collective-permute-start.10
  126.1 5.4 %shard_map.108 = bf16[8192,128]{1,0:T(8,128)(2,1)S(1)} custom-call(bf16[8,128,512]{2,1,0:T(8,128)(2,1)S(1)} %get-tuple-element.47.grad_ref, bf16[1024,4096]{1,0:T(8,128)(2,1)S(1)} %bitcast.21, s32[128,64]{1,0:T(8,128)S(1)} %copy-done.17), custom_call_target="tpu_custom_call" | custom-call | flops 3221225472 | bytes 12582912 | tf_op jit(solution)/shard_map/pallas_call | solution.py:415
  132.9 12.4 %all-to-all-start.2 = ((bf16[128,64,128]{2,1,0:T(8,128)(2,1)}), bf16[128,64,128]{2,1,0:T(8,128)(2,1)S(1)}, u32[]{:S(2)}, u32[]{:S(2)}) async-start(bf16[128,64,128]{2,1,0:T(8,128)(2,1)} %bitcast.24), calls=%async_computation.2 | async-start | bytes 4194304 | tf_op jit(solution)/shard_map/all_to_all | solution.py:425
  149.8 2.4 %collective-permute-start.12 = (bf16[256,512]{1,0:T(8,128)(2,1)S(1)}, bf16[256,512]{1,0:T(8,128)(2,1)S(1)}, u32[]{:S(2)}, u32[]{:S(2)}) collective-permute-start(bf16[256,512]{1,0:T(8,128)(2,1)S(1)} %get-tuple-element.59), channel_id=1, source_target_pairs={{0,4},{1,5},{2,6},{3,7},{4,0},{5,1},{6,2},{7,3},{8,12},{9,13},{10,... | collective-permute-start | bytes 786440 | tf_op jit(solution)/shard_map/ppermute | solution.py:430
  154.5 7.2 %collective-permute-done.11.refs_3_ = bf16[256,512]{1,0:T(8,128)(2,1)S(1)} collective-permute-done((bf16[256,512]{1,0:T(8,128)(2,1)S(1)}, bf16[256,512]{1,0:T(8,128)(2,1)S(1)}, u32[]{:S(2)}, u32[]{:S(2)}) %collective-permute-start.11) | collective-permute-done | bytes 262176 | tf_op jit(solution)/shard_map/ppermute | solution.py:430
  161.7 10.1 %collective-permute-done.12.refs_4_ = bf16[256,512]{1,0:T(8,128)(2,1)S(1)} collective-permute-done((bf16[256,512]{1,0:T(8,128)(2,1)S(1)}, bf16[256,512]{1,0:T(8,128)(2,1)S(1)}, u32[]{:S(2)}, u32[]{:S(2)}) %collective-permute-start.12) | collective-permute-done | bytes 262176 | tf_op jit(solution)/shard_map/ppermute | solution.py:430
  171.7 1.7 collective-permute-done.13.refs_5_
  173.4 1.8 shard_map.110
  177.4 19.2 %collective-permute-done.14.theirs_ref = bf16[528,512]{1,0:T(8,128)(2,1)S(1)} collective-permute-done((bf16[528,512]{1,0:T(8,128)(2,1)S(1)}, bf16[528,512]{1,0:T(8,128)(2,1)S(1)}, u32[]{:S(2)}, u32[]{:S(2)}) %collective-permute-start.14) | collective-permute-done | bytes 540704 | tf_op jit(solution)/shard_map/ppermute | solution.py:445
  197.6 10.8 %all-to-all-start.3 = ((bf16[64,40,128]{2,1,0:T(8,128)(2,1)}), bf16[64,40,128]{2,1,0:T(8,128)(2,1)S(1)}, u32[]{:S(2)}, u32[]{:S(2)}) async-start(bf16[64,40,128]{2,1,0:T(8,128)(2,1)} %bitcast.14), calls=%async_computation.3 | async-start | bytes 1310720 | tf_op jit(solution)/shard_map/all_to_all | solution.py:450
  209.1 11.2 %shard_map.113 = bf16[4096,128]{1,0:T(8,128)(2,1)} custom-call(s32[128,1,128]{2,1,0:T(1,128)S(1)} %copy-done.10, bf16[8192,128]{1,0:T(8,128)(2,1)S(1)} %bitcast.23), custom_call_target="tpu_custom_call" | custom-call | flops 8589934592 | bytes 4194304 | tf_op jit(solution)/shard_map/pallas_call | solution.py:458
  220.3 8.5 %all-to-all-done.3 = bf16[64,40,128]{2,1,0:T(8,128)(2,1)S(1)} async-done(((bf16[64,40,128]{2,1,0:T(8,128)(2,1)}), bf16[64,40,128]{2,1,0:T(8,128)(2,1)S(1)}, u32[]{:S(2)}, u32[]{:S(2)}) %all-to-all-start.3) | async-done | bytes 655392 | tf_op jit(solution)/shard_map/all_to_all | solution.py:450
  (87 shorter events, 20.9 us)
Async XLA Ops:
  2.0 33.0 %copy-start.13 = (bf16[4096,128]{1,0:T(8,128)(2,1)S(1)}, bf16[4096,128]{1,0:T(8,128)(2,1)}, u32[]{:S(2)}) copy-start(bf16[4096,128]{1,0:T(8,128)(2,1)} %table_ref.1) | copy-start | bytes 3145732
  7.4 92.9 %collective-permute-start.1 = (bf16[512,4096]{1,0:T(8,128)(2,1)}, bf16[512,4096]{1,0:T(8,128)(2,1)}, u32[]{:S(2)}, u32[]{:S(2)}) collective-permute-start(bf16[512,4096]{1,0:T(8,128)(2,1)} %get-tuple-element.40), channel_id=1, source_target_pairs={{0,136},{1,137},{2,138},{3,139},{4,140},{5,141},{6,142},{7,143},{8... | collective-permute-start | bytes 12582920 | tf_op jit(solution)/shard_map/ppermute | solution.py:366
  45.4 57.5 %copy-start.16 = (s32[128,64]{1,0:T(8,128)S(1)}, s32[128,64]{1,0:T(8,128)}, u32[]{:S(2)}) copy-start(s32[128,64]{1,0:T(8,128)} %get-tuple-element.38.bag_t_ref) | copy-start | bytes 98308
  45.4 57.5 %copy-start.18 = (s32[64,128]{1,0:T(8,128)S(1)}, s32[64,128]{1,0:T(8,128)}, u32[]{:S(2)}) copy-start(s32[64,128]{1,0:T(8,128)} %get-tuple-element.37.bag_ref) | copy-start | bytes 98308
  45.4 57.5 %all-to-all-start.1 = ((bf16[128,64,128]{2,1,0:T(8,128)(2,1)}), bf16[128,64,128]{2,1,0:T(8,128)(2,1)S(1)}, u32[]{:S(2)}, u32[]{:S(2)}) async-start(bf16[128,64,128]{2,1,0:T(8,128)(2,1)} %bitcast.26), calls=%async_computation.1 | async-start | bytes 4194304 | tf_op jit(solution)/shard_map/all_to_all | solution.py:376
  100.3 18.0 %collective-permute-start.2 = (bf16[512,4096]{1,0:T(8,128)(2,1)}, bf16[512,4096]{1,0:T(8,128)(2,1)}, u32[]{:S(2)}, u32[]{:S(2)}) collective-permute-start(bf16[512,4096]{1,0:T(8,128)(2,1)} %collective-permute-done.1.w_near_ref), channel_id=1, source_target_pairs={{0,1},{1,0},{2,3},{3,2},{4,5},{5,4},{6,7},{7,6},{8,9},{9,8},{10,11... | collective-permute-start | bytes 12582920 | tf_op jit(solution)/shard_map/ppermute | solution.py:367
  106.6 11.7 %collective-permute-start = (bf16[128,1024]{1,0:T(8,128)(2,1)S(1)}, bf16[128,1024]{1,0:T(8,128)(2,1)S(1)}, u32[]{:S(2)}, u32[]{:S(2)}) collective-permute-start(bf16[128,1024]{1,0:T(8,128)(2,1)S(1)} %shard_map.104.pooled_ref.refs_0_), channel_id=1, source_target_pairs={{0,128},{128,0},{1,129},{129,1},{2,130},{130,2},{3,131},{131,3},{4... | collective-permute-start | bytes 786440 | tf_op jit(solution)/shard_map/ppermute | solution.py:386
  108.6 17.4 %collective-permute-start.4 = (bf16[128,1024]{1,0:T(8,128)(2,1)S(1)}, bf16[128,1024]{1,0:T(8,128)(2,1)S(1)}, u32[]{:S(2)}, u32[]{:S(2)}) collective-permute-start(bf16[128,1024]{1,0:T(8,128)(2,1)S(1)} %shard_map.104.pooled_ref.refs_0_), channel_id=1, source_target_pairs={{0,2},{1,3},{2,4},{3,5},{4,6},{5,7},{6,0},{7,1},{8,10},{9,11},{10,... | collective-permute-start | bytes 786440 | tf_op jit(solution)/shard_map/ppermute | solution.py:391
  109.9 16.1 %collective-permute-start.5 = (bf16[128,1024]{1,0:T(8,128)(2,1)S(1)}, bf16[128,1024]{1,0:T(8,128)(2,1)S(1)}, u32[]{:S(2)}, u32[]{:S(2)}) collective-permute-start(bf16[128,1024]{1,0:T(8,128)(2,1)S(1)} %shard_map.104.pooled_ref.refs_0_), channel_id=1, source_target_pairs={{0,4},{1,5},{2,6},{3,7},{4,0},{5,1},{6,2},{7,3},{8,12},{9,13},{10,... | collective-permute-start | bytes 786440 | tf_op jit(solution)/shard_map/ppermute | solution.py:391
  112.5 13.5 %collective-permute-start.6 = (bf16[128,1024]{1,0:T(8,128)(2,1)S(1)}, bf16[128,1024]{1,0:T(8,128)(2,1)S(1)}, u32[]{:S(2)}, u32[]{:S(2)}) collective-permute-start(bf16[128,1024]{1,0:T(8,128)(2,1)S(1)} %shard_map.104.pooled_ref.refs_0_), channel_id=1, source_target_pairs={{0,6},{1,7},{2,0},{3,1},{4,2},{5,3},{6,4},{7,5},{8,14},{9,15},{10,... | collective-permute-start | bytes 786440 | tf_op jit(solution)/shard_map/ppermute | solution.py:391
  124.4 8.5 %collective-permute-start.10 = (bf16[4,128,512]{2,1,0:T(8,128)(2,1)S(1)}, bf16[4,128,512]{2,1,0:T(8,128)(2,1)S(1)}, u32[]{:S(2)}, u32[]{:S(2)}) collective-permute-start(bf16[4,128,512]{2,1,0:T(8,128)(2,1)S(1)} %get-tuple-element.48), channel_id=1, source_target_pairs={{0,1},{1,0},{2,3},{3,2},{4,5},{5,4},{6,7},{7,6},{8,9},{9,8},{10,11... | collective-permute-start | bytes 1572872 | tf_op jit(solution)/shard_map/ppermute | solution.py:423
  132.9 64.7 %all-to-all-start.2 = ((bf16[128,64,128]{2,1,0:T(8,128)(2,1)}), bf16[128,64,128]{2,1,0:T(8,128)(2,1)S(1)}, u32[]{:S(2)}, u32[]{:S(2)}) async-start(bf16[128,64,128]{2,1,0:T(8,128)(2,1)} %bitcast.24), calls=%async_computation.2 | async-start | bytes 4194304 | tf_op jit(solution)/shard_map/all_to_all | solution.py:425
  145.3 4.4 %collective-permute-start.3 = (bf16[128,1024]{1,0:T(8,128)(2,1)S(1)}, bf16[128,1024]{1,0:T(8,128)(2,1)S(1)}, u32[]{:S(2)}, u32[]{:S(2)}) collective-permute-start(bf16[128,1024]{1,0:T(8,128)(2,1)S(1)} %shard_map.104.pooled_ref.refs_0_), channel_id=1, source_target_pairs={{0,1},{1,0},{2,3},{3,2},{4,5},{5,4},{6,7},{7,6},{8,9},{9,8},{10,11... | collective-permute-start | bytes 786440 | tf_op jit(solution)/shard_map/ppermute | solution.py:413
  146.3 5.9 %collective-permute-start.7 = (bf16[128,1024]{1,0:T(8,128)(2,1)S(1)}, bf16[128,1024]{1,0:T(8,128)(2,1)S(1)}, u32[]{:S(2)}, u32[]{:S(2)}) collective-permute-start(bf16[128,1024]{1,0:T(8,128)(2,1)S(1)} %collective-permute-done.4.refs_2_), channel_id=1, source_target_pairs={{0,1},{1,0},{2,3},{3,2},{4,5},{5,4},{6,7},{7,6},{8,9},{9,8},{10,11... | collective-permute-start | bytes 786440 | tf_op jit(solution)/shard_map/ppermute | solution.py:413
  146.4 6.9 %collective-permute-start.8 = (bf16[128,1024]{1,0:T(8,128)(2,1)S(1)}, bf16[128,1024]{1,0:T(8,128)(2,1)S(1)}, u32[]{:S(2)}, u32[]{:S(2)}) collective-permute-start(bf16[128,1024]{1,0:T(8,128)(2,1)S(1)} %collective-permute-done.5.refs_4_), channel_id=1, source_target_pairs={{0,1},{1,0},{2,3},{3,2},{4,5},{5,4},{6,7},{7,6},{8,9},{9,8},{10,11... | collective-permute-start | bytes 786440 | tf_op jit(solution)/shard_map/ppermute | solution.py:413
  146.8 6.5 %collective-permute-start.9 = (bf16[128,1024]{1,0:T(8,128)(2,1)}, bf16[128,1024]{1,0:T(8,128)(2,1)S(1)}, u32[]{:S(2)}, u32[]{:S(2)}) collective-permute-start(bf16[128,1024]{1,0:T(8,128)(2,1)} %copy-done.3), channel_id=1, source_target_pairs={{0,1},{1,0},{2,3},{3,2},{4,5},{5,4},{6,7},{7,6},{8,9},{9,8},{10,11... | collective-permute-start | bytes 786440 | tf_op jit(solution)/shard_map/ppermute | solution.py:413
  148.8 12.9 %collective-permute-start.11 = (bf16[256,512]{1,0:T(8,128)(2,1)S(1)}, bf16[256,512]{1,0:T(8,128)(2,1)S(1)}, u32[]{:S(2)}, u32[]{:S(2)}) collective-permute-start(bf16[256,512]{1,0:T(8,128)(2,1)S(1)} %get-tuple-element.58), channel_id=1, source_target_pairs={{0,2},{1,3},{2,4},{3,5},{4,6},{5,7},{6,0},{7,1},{8,10},{9,11},{10,... | collective-permute-start | bytes 786440 | tf_op jit(solution)/shard_map/ppermute | solution.py:430
  149.8 22.0 %collective-permute-start.12 = (bf16[256,512]{1,0:T(8,128)(2,1)S(1)}, bf16[256,512]{1,0:T(8,128)(2,1)S(1)}, u32[]{:S(2)}, u32[]{:S(2)}) collective-permute-start(bf16[256,512]{1,0:T(8,128)(2,1)S(1)} %get-tuple-element.59), channel_id=1, source_target_pairs={{0,4},{1,5},{2,6},{3,7},{4,0},{5,1},{6,2},{7,3},{8,12},{9,13},{10,... | collective-permute-start | bytes 786440 | tf_op jit(solution)/shard_map/ppermute | solution.py:430
  152.2 21.3 %collective-permute-start.13 = (bf16[256,512]{1,0:T(8,128)(2,1)S(1)}, bf16[256,512]{1,0:T(8,128)(2,1)S(1)}, u32[]{:S(2)}, u32[]{:S(2)}) collective-permute-start(bf16[256,512]{1,0:T(8,128)(2,1)S(1)} %get-tuple-element.60), channel_id=1, source_target_pairs={{0,6},{1,7},{2,0},{3,1},{4,2},{5,3},{6,4},{7,5},{8,14},{9,15},{10,... | collective-permute-start | bytes 786440 | tf_op jit(solution)/shard_map/ppermute | solution.py:430
  154.4 22.0 %copy-start.12 = (f32[128,1]{1,0:T(8,128)S(1)}, f32[128,1]{1,0:T(8,128)}, u32[]{:S(2)}) copy-start(f32[128,1]{1,0:T(8,128)} %copy-done.11) | copy-start | bytes 1540
  175.3 33.8 %copy-start.10 = (s32[128,1,128]{2,1,0:T(1,128)S(1)}, s32[128,1,128]{2,1,0:T(1,128)}, u32[]{:S(2)}) copy-start(s32[128,1,128]{2,1,0:T(1,128)} %copy-done.9) | copy-start | bytes 196612
  175.3 21.3 %collective-permute-start.14 = (bf16[528,512]{1,0:T(8,128)(2,1)S(1)}, bf16[528,512]{1,0:T(8,128)(2,1)S(1)}, u32[]{:S(2)}, u32[]{:S(2)}) collective-permute-start(bf16[528,512]{1,0:T(8,128)(2,1)S(1)} %get-tuple-element.63), channel_id=1, source_target_pairs={{0,8},{1,9},{2,10},{3,11},{4,12},{5,13},{6,14},{7,15},{8,0},{9,1},... | collective-permute-start | bytes 1622024 | tf_op jit(solution)/shard_map/ppermute | solution.py:445
  176.5 21.1 %collective-permute-start.15 = (f32[128,1]{1,0:T(8,128)S(1)}, f32[128,1]{1,0:T(8,128)S(1)}, u32[]{:S(2)}, u32[]{:S(2)}) collective-permute-start(f32[128,1]{1,0:T(8,128)S(1)} %copy-done.12), channel_id=1, source_target_pairs={{0,128},{128,0},{1,129},{129,1},{2,130},{130,2},{3,131},{131,3},{4... | collective-permute-start | bytes 1544 | tf_op jit(solution)/shard_map/ppermute | solution.py:448
  197.6 31.2 %all-to-all-start.3 = ((bf16[64,40,128]{2,1,0:T(8,128)(2,1)}), bf16[64,40,128]{2,1,0:T(8,128)(2,1)S(1)}, u32[]{:S(2)}, u32[]{:S(2)}) async-start(bf16[64,40,128]{2,1,0:T(8,128)(2,1)} %bitcast.14), calls=%async_computation.3 | async-start | bytes 1310720 | tf_op jit(solution)/shard_map/all_to_all | solution.py:450
  (20 other events, 133.3 us)

commit v3 on v2

--- a/solution.py
+++ b/solution.py
@@ -148,11 +148,7 @@
 
 
 def part_kernel(pooled_ref, w_ref, part_ref):
-    step = 512
-    for j in range(w_ref.shape[1] // step):
-        part_ref[:, j * step : (j + 1) * step] = jnp.dot(
-            pooled_ref[...], w_ref[:, j * step : (j + 1) * step], preferred_element_type=F32
-        )
+    part_ref[...] = jnp.dot(pooled_ref[...], w_ref[...], preferred_element_type=F32)
 
 
 def peer(where_ref, e, sign):
@@ -384,8 +380,17 @@
         [pltpu.VMEM((slots, E), BF16), pltpu.VMEM((LOW, bags // LOW * E), F32)],
     )(bag, bag_t, returned)
     other = lax.ppermute(pooled, "grp", [(0, 1), (1, 0)])
-    part = call(
-        part_kernel, shape((samples, hidden_width), F32), 2 * samples * feats * hidden_width, 10 << 20, mib=20
+    step = hidden_width // 8
+    part = pl.pallas_call(
+        part_kernel,
+        out_shape=shape((samples, hidden_width), F32),
+        grid=(8,),
+        in_specs=[pl.BlockSpec((samples, feats), lambda j: (0, 0)), pl.BlockSpec((feats, step), lambda j: (0, j))],
+        out_specs=pl.BlockSpec((samples, step), lambda j: (0, j)),
+        compiler_params=pltpu.CompilerParams(vmem_limit_bytes=56 << 20),
+        cost_estimate=pl.CostEstimate(
+            flops=2 * samples * feats * hidden_width, bytes_accessed=10 << 20, transcendentals=0
+        ),
     )(pooled, w_first)
 
     side_pooled = [lax.ppermute(pooled, "wa", to_peer[2 * d]) for d in range(1, 4)]

time: 236 us -> 241 us (1.021)
  Pallas kernels: 45.8 us -> 53.1 us
  starting transfers between devices: 51.7 us -> 49.2 us
    pallas_call x1, Pallas kernels: 1.27 us -> 8.52 us  [shards(): pl.pallas_call(part_kernel, out_shape=shape((samples, hidden_width), F32)...]
    unnamed x50 -> x54, local copies, waits for them, and re-layouts: 8.86 us -> 7.87 us
  transfers between devices with their start and end apart: 19 -> 19, of which waited for: 7 -> 7; matrix products, arithmetic and copies ran while one was open for 0% -> 0% of each run, Pallas kernels for 17% -> 20%
where the time goes in v3:
time: 241 us; the launch traced here: 236 us
  waiting for transfers between devices  96.2 us (40%)
  Pallas kernels  53.1 us (22%)
  starting transfers between devices  49.2 us (20%)
  blocking collectives  24.5 us (10%)
  local copies, waits for them, and re-layouts  9.19 us (4%)
  other arithmetic  2.64 us (1%)
    ppermute x1, waiting for transfers between devices, shards(): near_half = lax.ppermute(near_half, ('grp', 'wa'), across)  48.5 us
    all_to_all x1, blocking collectives, shards(): ids_in = lax.all_to_all(ids, 'wa', split_axis=0, concat_axis=0, tiled=True)  24.5 us
    ppermute x1, waiting for transfers between devices, shards(): theirs = lax.ppermute(theirs, 'wa', to_x)  19.6 us
    ppermute x3, waiting for transfers between devices, shards(): lax.ppermute(packed[d - 1], 'wa', to_peer[2 * d])  19 us
    all_to_all x1, starting transfers between devices, shards(): lax.all_to_all(send.reshape(count, CAP, E), 'wa', split_axis=0, concat_ax...  11.4 us
    pallas_call x1, Pallas kernels, shards(): call(scatter_kernel, shape((table.shape[0], E), BF16), 2 * slots * 4096 *...  11.2 us
    all_to_all x1, starting transfers between devices, shards(): lax.all_to_all(laid.reshape(8 * planes, size, E), 'wa', 0, 0, axis_index_...  10.3 us
    pallas_call x1, Pallas kernels, shards(): call(gather_kernel, shape((slots, E), BF16), 2 * slots * 4096 * E, 4 << 2...  9.15 us
  transfers between devices with their start and end apart: 19, of which 7 were waited for; matrix products, arithmetic and copies ran while one was open for 0% of the time, Pallas kernels for 20%

profile of v3, /device:TPU:1, one launch (start us, length us, event | category | flops | bytes accessed | tf_op | source)
XLA Modules:
  0.0 236.1 jit_solution(13805155442090483784)
XLA Ops:
  2.0 5.4 %shard_map.102 = (s32[128,1,128]{2,1,0:T(1,128)}, s32[64,128]{1,0:T(8,128)}, s32[128,64]{1,0:T(8,128)}, bf16[512,4096]{1,0:T(8,128)(2,1)}) custom-call(s32[32,128]{1,0:T(8,128)} %bitcast.27, bf16[1024,4096]{1,0:T(8,128)(2,1)} %w_ref.5), custom_call_target="tpu_custom_call" | custom-call | flops 1073741824 | bytes 8388608 | tf_op jit(solution)/shard_map/pallas_call | solution.py:348
  7.4 3.4 %collective-permute-start.1 = (bf16[512,4096]{1,0:T(8,128)(2,1)}, bf16[512,4096]{1,0:T(8,128)(2,1)}, u32[]{:S(2)}, u32[]{:S(2)}) collective-permute-start(bf16[512,4096]{1,0:T(8,128)(2,1)} %get-tuple-element.40), channel_id=1, source_target_pairs={{0,136},{1,137},{2,138},{3,139},{4,140},{5,141},{6,142},{7,143},{8... | collective-permute-start | bytes 12582920 | tf_op jit(solution)/shard_map/ppermute | solution.py:362
  10.8 24.5 %all_to_all.20.ids_ref = s32[128,1,128]{2,1,0:T(1,128)S(1)} all-to-all(s32[128,1,128]{2,1,0:T(1,128)} %get-tuple-element.39), channel_id=1, replica_groups=mesh['grp'=2,'wa'=128] {'wa'}, dimensions={0} | all-to-all | bytes 131072 | tf_op jit(solution)/shard_map/all_to_all | solution.py:364
  35.3 9.1 %shard_map.103 = bf16[8192,128]{1,0:T(8,128)(2,1)S(1)} custom-call(s32[128,1,128]{2,1,0:T(1,128)S(1)} %all_to_all.20.ids_ref, bf16[4096,128]{1,0:T(8,128)(2,1)S(1)} %copy-done.15), custom_call_target="tpu_custom_call" | custom-call | flops 8589934592 | bytes 4194304 | tf_op jit(solution)/shard_map/pallas_call | solution.py:365
  45.8 6.0 %all-to-all-start.1 = ((bf16[128,64,128]{2,1,0:T(8,128)(2,1)}), bf16[128,64,128]{2,1,0:T(8,128)(2,1)S(1)}, u32[]{:S(2)}, u32[]{:S(2)}) async-start(bf16[128,64,128]{2,1,0:T(8,128)(2,1)} %bitcast.26), calls=%async_computation.1 | async-start | bytes 4194304 | tf_op jit(solution)/shard_map/all_to_all | solution.py:372
  51.8 48.5 %collective-permute-done.1.w_near_ref = bf16[512,4096]{1,0:T(8,128)(2,1)} collective-permute-done((bf16[512,4096]{1,0:T(8,128)(2,1)}, bf16[512,4096]{1,0:T(8,128)(2,1)}, u32[]{:S(2)}, u32[]{:S(2)}) %collective-permute-start.1) | collective-permute-done | bytes 4194336 | tf_op jit(solution)/shard_map/ppermute | solution.py:362
  100.3 2.4 %collective-permute-start.2 = (bf16[512,4096]{1,0:T(8,128)(2,1)}, bf16[512,4096]{1,0:T(8,128)(2,1)}, u32[]{:S(2)}, u32[]{:S(2)}) collective-permute-start(bf16[512,4096]{1,0:T(8,128)(2,1)} %collective-permute-done.1.w_near_ref), channel_id=1, source_target_pairs={{0,1},{1,0},{2,3},{3,2},{4,5},{5,4},{6,7},{7,6},{8,9},{9,8},{10,11... | collective-permute-start | bytes 12582920 | tf_op jit(solution)/shard_map/ppermute | solution.py:363
  103.3 3.7 %shard_map.104.pooled_ref.refs_0_ = bf16[128,1024]{1,0:T(8,128)(2,1)S(1)} custom-call(s32[64,128]{1,0:T(8,128)S(1)} %copy-done.20, s32[128,64]{1,0:T(8,128)S(1)} %copy-done.18, bf16[8192,128]{1,0:T(8,128)(2,1)S(1)} %bitcast.25), custom_call_target="tpu_custom_call" | custom-call | flops 2147483648 | bytes 4194304 | tf_op jit(solution)/shard_map/pallas_call | solution.py:375
  109.9 2.6 %collective-permute-start.5 = (bf16[128,1024]{1,0:T(8,128)(2,1)S(1)}, bf16[128,1024]{1,0:T(8,128)(2,1)S(1)}, u32[]{:S(2)}, u32[]{:S(2)}) collective-permute-start(bf16[128,1024]{1,0:T(8,128)(2,1)S(1)} %shard_map.104.pooled_ref.refs_0_), channel_id=1, source_target_pairs={{0,4},{1,5},{2,6},{3,7},{4,0},{5,1},{6,2},{7,3},{8,12},{9,13},{10,... | collective-permute-start | bytes 786440 | tf_op jit(solution)/shard_map/ppermute | solution.py:396
  113.6 8.5 %shard_map.105.part_ref = f32[128,4096]{1,0:T(8,128)} custom-call(bf16[128,1024]{1,0:T(8,128)(2,1)} %copy-done.3, bf16[1024,4096]{1,0:T(8,128)(2,1)} %w_ref.5), custom_call_target="tpu_custom_call" | custom-call | flops 1073741824 | bytes 10485760 | tf_op jit(solution)/shard_map/pallas_call | solution.py:384
  122.1 1.7 copy-done
  123.9 6.0 %shard_map.106 = (f32[128,1]{1,0:T(8,128)S(1)}, f32[1,4096]{1,0:T(1,128)S(1)}, bf16[8,128,512]{2,1,0:T(8,128)(2,1)S(1)}, bf16[4,128,512]{2,1,0:T(8,128)(2,1)S(1)...) custom-call(s32[5]{0:T(128)S(1)} %stack.23.where_ref, ...), custom_call_target="tpu_custom_call" | custom-call | flops 1105199104 | bytes 4194304 | tf_op jit(solution)/shard_map/pallas_call | solution.py:399
  130.5 1.5 collective-permute-start.10
  132.0 5.4 %shard_map.108 = bf16[8192,128]{1,0:T(8,128)(2,1)S(1)} custom-call(bf16[8,128,512]{2,1,0:T(8,128)(2,1)S(1)} %get-tuple-element.47.grad_ref, bf16[1024,4096]{1,0:T(8,128)(2,1)S(1)} %bitcast.21, s32[128,64]{1,0:T(8,128)S(1)} %copy-done.19), custom_call_target="tpu_custom_call" | custom-call | flops 3221225472 | bytes 12582912 | tf_op jit(solution)/shard_map/pallas_call | solution.py:420
  138.9 11.4 %all-to-all-start.2 = ((bf16[128,64,128]{2,1,0:T(8,128)(2,1)}), bf16[128,64,128]{2,1,0:T(8,128)(2,1)S(1)}, u32[]{:S(2)}, u32[]{:S(2)}) async-start(bf16[128,64,128]{2,1,0:T(8,128)(2,1)} %bitcast.24), calls=%async_computation.2 | async-start | bytes 4194304 | tf_op jit(solution)/shard_map/all_to_all | solution.py:430
  154.7 2.4 %collective-permute-start.12 = (bf16[256,512]{1,0:T(8,128)(2,1)S(1)}, bf16[256,512]{1,0:T(8,128)(2,1)S(1)}, u32[]{:S(2)}, u32[]{:S(2)}) collective-permute-start(bf16[256,512]{1,0:T(8,128)(2,1)S(1)} %get-tuple-element.59), channel_id=1, source_target_pairs={{0,4},{1,5},{2,6},{3,7},{4,0},{5,1},{6,2},{7,3},{8,12},{9,13},{10,... | collective-permute-start | bytes 786440 | tf_op jit(solution)/shard_map/ppermute | solution.py:435
  159.4 7.2 %collective-permute-done.11.refs_3_ = bf16[256,512]{1,0:T(8,128)(2,1)S(1)} collective-permute-done((bf16[256,512]{1,0:T(8,128)(2,1)S(1)}, bf16[256,512]{1,0:T(8,128)(2,1)S(1)}, u32[]{:S(2)}, u32[]{:S(2)}) %collective-permute-start.11) | collective-permute-done | bytes 262176 | tf_op jit(solution)/shard_map/ppermute | solution.py:435
  166.7 10.0 %collective-permute-done.12.refs_4_ = bf16[256,512]{1,0:T(8,128)(2,1)S(1)} collective-permute-done((bf16[256,512]{1,0:T(8,128)(2,1)S(1)}, bf16[256,512]{1,0:T(8,128)(2,1)S(1)}, u32[]{:S(2)}, u32[]{:S(2)}) %collective-permute-start.12) | collective-permute-done | bytes 262176 | tf_op jit(solution)/shard_map/ppermute | solution.py:435
  176.7 1.7 collective-permute-done.13.refs_5_
  178.4 1.8 shard_map.110
  182.0 19.6 %collective-permute-done.14.theirs_ref = bf16[528,512]{1,0:T(8,128)(2,1)S(1)} collective-permute-done((bf16[528,512]{1,0:T(8,128)(2,1)S(1)}, bf16[528,512]{1,0:T(8,128)(2,1)S(1)}, u32[]{:S(2)}, u32[]{:S(2)}) %collective-permute-start.14) | collective-permute-done | bytes 540704 | tf_op jit(solution)/shard_map/ppermute | solution.py:450
  202.6 10.3 %all-to-all-start.3 = ((bf16[64,40,128]{2,1,0:T(8,128)(2,1)}), bf16[64,40,128]{2,1,0:T(8,128)(2,1)S(1)}, u32[]{:S(2)}, u32[]{:S(2)}) async-start(bf16[64,40,128]{2,1,0:T(8,128)(2,1)} %bitcast.14), calls=%async_computation.3 | async-start | bytes 1310720 | tf_op jit(solution)/shard_map/all_to_all | solution.py:455
  213.6 11.2 %shard_map.113 = bf16[4096,128]{1,0:T(8,128)(2,1)} custom-call(s32[128,1,128]{2,1,0:T(1,128)S(1)} %copy-done.12, bf16[8192,128]{1,0:T(8,128)(2,1)S(1)} %bitcast.23), custom_call_target="tpu_custom_call" | custom-call | flops 8589934592 | bytes 4194304 | tf_op jit(solution)/shard_map/pallas_call | solution.py:463
  224.8 8.5 %all-to-all-done.3 = bf16[64,40,128]{2,1,0:T(8,128)(2,1)S(1)} async-done(((bf16[64,40,128]{2,1,0:T(8,128)(2,1)}), bf16[64,40,128]{2,1,0:T(8,128)(2,1)S(1)}, u32[]{:S(2)}, u32[]{:S(2)}) %all-to-all-start.3) | async-done | bytes 655392 | tf_op jit(solution)/shard_map/all_to_all | solution.py:455
  (91 shorter events, 21.7 us)
Async XLA Ops:
  2.0 33.3 %copy-start.15 = (bf16[4096,128]{1,0:T(8,128)(2,1)S(1)}, bf16[4096,128]{1,0:T(8,128)(2,1)}, u32[]{:S(2)}) copy-start(bf16[4096,128]{1,0:T(8,128)(2,1)} %table_ref.1) | copy-start | bytes 3145732
  7.4 93.0 %collective-permute-start.1 = (bf16[512,4096]{1,0:T(8,128)(2,1)}, bf16[512,4096]{1,0:T(8,128)(2,1)}, u32[]{:S(2)}, u32[]{:S(2)}) collective-permute-start(bf16[512,4096]{1,0:T(8,128)(2,1)} %get-tuple-element.40), channel_id=1, source_target_pairs={{0,136},{1,137},{2,138},{3,139},{4,140},{5,141},{6,142},{7,143},{8... | collective-permute-start | bytes 12582920 | tf_op jit(solution)/shard_map/ppermute | solution.py:362
  45.8 57.5 %copy-start.18 = (s32[128,64]{1,0:T(8,128)S(1)}, s32[128,64]{1,0:T(8,128)}, u32[]{:S(2)}) copy-start(s32[128,64]{1,0:T(8,128)} %get-tuple-element.38.bag_t_ref) | copy-start | bytes 98308
  45.8 57.5 %copy-start.20 = (s32[64,128]{1,0:T(8,128)S(1)}, s32[64,128]{1,0:T(8,128)}, u32[]{:S(2)}) copy-start(s32[64,128]{1,0:T(8,128)} %get-tuple-element.37.bag_ref) | copy-start | bytes 98308
  45.8 57.5 %all-to-all-start.1 = ((bf16[128,64,128]{2,1,0:T(8,128)(2,1)}), bf16[128,64,128]{2,1,0:T(8,128)(2,1)S(1)}, u32[]{:S(2)}, u32[]{:S(2)}) async-start(bf16[128,64,128]{2,1,0:T(8,128)(2,1)} %bitcast.26), calls=%async_computation.1 | async-start | bytes 4194304 | tf_op jit(solution)/shard_map/all_to_all | solution.py:372
  100.3 21.8 %collective-permute-start.2 = (bf16[512,4096]{1,0:T(8,128)(2,1)}, bf16[512,4096]{1,0:T(8,128)(2,1)}, u32[]{:S(2)}, u32[]{:S(2)}) collective-permute-start(bf16[512,4096]{1,0:T(8,128)(2,1)} %collective-permute-done.1.w_near_ref), channel_id=1, source_target_pairs={{0,1},{1,0},{2,3},{3,2},{4,5},{5,4},{6,7},{7,6},{8,9},{9,8},{10,11... | collective-permute-start | bytes 12582920 | tf_op jit(solution)/shard_map/ppermute | solution.py:363
  107.0 15.1 %collective-permute-start = (bf16[128,1024]{1,0:T(8,128)(2,1)S(1)}, bf16[128,1024]{1,0:T(8,128)(2,1)S(1)}, u32[]{:S(2)}, u32[]{:S(2)}) collective-permute-start(bf16[128,1024]{1,0:T(8,128)(2,1)S(1)} %shard_map.104.pooled_ref.refs_0_), channel_id=1, source_target_pairs={{0,128},{128,0},{1,129},{129,1},{2,130},{130,2},{3,131},{131,3},{4... | collective-permute-start | bytes 786440 | tf_op jit(solution)/shard_map/ppermute | solution.py:382
  108.6 23.4 %collective-permute-start.4 = (bf16[128,1024]{1,0:T(8,128)(2,1)S(1)}, bf16[128,1024]{1,0:T(8,128)(2,1)S(1)}, u32[]{:S(2)}, u32[]{:S(2)}) collective-permute-start(bf16[128,1024]{1,0:T(8,128)(2,1)S(1)} %shard_map.104.pooled_ref.refs_0_), channel_id=1, source_target_pairs={{0,2},{1,3},{2,4},{3,5},{4,6},{5,7},{6,0},{7,1},{8,10},{9,11},{10,... | collective-permute-start | bytes 786440 | tf_op jit(solution)/shard_map/ppermute | solution.py:396
  109.9 22.1 %collective-permute-start.5 = (bf16[128,1024]{1,0:T(8,128)(2,1)S(1)}, bf16[128,1024]{1,0:T(8,128)(2,1)S(1)}, u32[]{:S(2)}, u32[]{:S(2)}) collective-permute-start(bf16[128,1024]{1,0:T(8,128)(2,1)S(1)} %shard_map.104.pooled_ref.refs_0_), channel_id=1, source_target_pairs={{0,4},{1,5},{2,6},{3,7},{4,0},{5,1},{6,2},{7,3},{8,12},{9,13},{10,... | collective-permute-start | bytes 786440 | tf_op jit(solution)/shard_map/ppermute | solution.py:396
  112.5 19.5 %collective-permute-start.6 = (bf16[128,1024]{1,0:T(8,128)(2,1)S(1)}, bf16[128,1024]{1,0:T(8,128)(2,1)S(1)}, u32[]{:S(2)}, u32[]{:S(2)}) collective-permute-start(bf16[128,1024]{1,0:T(8,128)(2,1)S(1)} %shard_map.104.pooled_ref.refs_0_), channel_id=1, source_target_pairs={{0,6},{1,7},{2,0},{3,1},{4,2},{5,3},{6,4},{7,5},{8,14},{9,15},{10,... | collective-permute-start | bytes 786440 | tf_op jit(solution)/shard_map/ppermute | solution.py:396
  130.5 8.3 %collective-permute-start.10 = (bf16[4,128,512]{2,1,0:T(8,128)(2,1)S(1)}, bf16[4,128,512]{2,1,0:T(8,128)(2,1)S(1)}, u32[]{:S(2)}, u32[]{:S(2)}) collective-permute-start(bf16[4,128,512]{2,1,0:T(8,128)(2,1)S(1)} %get-tuple-element.48), channel_id=1, source_target_pairs={{0,1},{1,0},{2,3},{3,2},{4,5},{5,4},{6,7},{7,6},{8,9},{9,8},{10,11... | collective-permute-start | bytes 1572872 | tf_op jit(solution)/shard_map/ppermute | solution.py:428
  138.9 63.7 %all-to-all-start.2 = ((bf16[128,64,128]{2,1,0:T(8,128)(2,1)}), bf16[128,64,128]{2,1,0:T(8,128)(2,1)S(1)}, u32[]{:S(2)}, u32[]{:S(2)}) async-start(bf16[128,64,128]{2,1,0:T(8,128)(2,1)} %bitcast.24), calls=%async_computation.2 | async-start | bytes 4194304 | tf_op jit(solution)/shard_map/all_to_all | solution.py:430
  150.3 4.4 %collective-permute-start.3 = (bf16[128,1024]{1,0:T(8,128)(2,1)S(1)}, bf16[128,1024]{1,0:T(8,128)(2,1)S(1)}, u32[]{:S(2)}, u32[]{:S(2)}) collective-permute-start(bf16[128,1024]{1,0:T(8,128)(2,1)S(1)} %copy-done.4), channel_id=1, source_target_pairs={{0,1},{1,0},{2,3},{3,2},{4,5},{5,4},{6,7},{7,6},{8,9},{9,8},{10,11... | collective-permute-start | bytes 786440 | tf_op jit(solution)/shard_map/ppermute | solution.py:418
  151.3 5.9 %collective-permute-start.7 = (bf16[128,1024]{1,0:T(8,128)(2,1)S(1)}, bf16[128,1024]{1,0:T(8,128)(2,1)S(1)}, u32[]{:S(2)}, u32[]{:S(2)}) collective-permute-start(bf16[128,1024]{1,0:T(8,128)(2,1)S(1)} %collective-permute-done.4.refs_2_), channel_id=1, source_target_pairs={{0,1},{1,0},{2,3},{3,2},{4,5},{5,4},{6,7},{7,6},{8,9},{9,8},{10,11... | collective-permute-start | bytes 786440 | tf_op jit(solution)/shard_map/ppermute | solution.py:418
  151.4 6.9 %collective-permute-start.8 = (bf16[128,1024]{1,0:T(8,128)(2,1)S(1)}, bf16[128,1024]{1,0:T(8,128)(2,1)S(1)}, u32[]{:S(2)}, u32[]{:S(2)}) collective-permute-start(bf16[128,1024]{1,0:T(8,128)(2,1)S(1)} %collective-permute-done.5.refs_4_), channel_id=1, source_target_pairs={{0,1},{1,0},{2,3},{3,2},{4,5},{5,4},{6,7},{7,6},{8,9},{9,8},{10,11... | collective-permute-start | bytes 786440 | tf_op jit(solution)/shard_map/ppermute | solution.py:418
  151.8 6.5 %collective-permute-start.9 = (bf16[128,1024]{1,0:T(8,128)(2,1)}, bf16[128,1024]{1,0:T(8,128)(2,1)S(1)}, u32[]{:S(2)}, u32[]{:S(2)}) collective-permute-start(bf16[128,1024]{1,0:T(8,128)(2,1)} %copy-done.5), channel_id=1, source_target_pairs={{0,1},{1,0},{2,3},{3,2},{4,5},{5,4},{6,7},{7,6},{8,9},{9,8},{10,11... | collective-permute-start | bytes 786440 | tf_op jit(solution)/shard_map/ppermute | solution.py:418
  153.7 12.9 %collective-permute-start.11 = (bf16[256,512]{1,0:T(8,128)(2,1)S(1)}, bf16[256,512]{1,0:T(8,128)(2,1)S(1)}, u32[]{:S(2)}, u32[]{:S(2)}) collective-permute-start(bf16[256,512]{1,0:T(8,128)(2,1)S(1)} %get-tuple-element.58), channel_id=1, source_target_pairs={{0,2},{1,3},{2,4},{3,5},{4,6},{5,7},{6,0},{7,1},{8,10},{9,11},{10,... | collective-permute-start | bytes 786440 | tf_op jit(solution)/shard_map/ppermute | solution.py:435
  154.7 22.0 %collective-permute-start.12 = (bf16[256,512]{1,0:T(8,128)(2,1)S(1)}, bf16[256,512]{1,0:T(8,128)(2,1)S(1)}, u32[]{:S(2)}, u32[]{:S(2)}) collective-permute-start(bf16[256,512]{1,0:T(8,128)(2,1)S(1)} %get-tuple-element.59), channel_id=1, source_target_pairs={{0,4},{1,5},{2,6},{3,7},{4,0},{5,1},{6,2},{7,3},{8,12},{9,13},{10,... | collective-permute-start | bytes 786440 | tf_op jit(solution)/shard_map/ppermute | solution.py:435
  157.1 21.3 %collective-permute-start.13 = (bf16[256,512]{1,0:T(8,128)(2,1)S(1)}, bf16[256,512]{1,0:T(8,128)(2,1)S(1)}, u32[]{:S(2)}, u32[]{:S(2)}) collective-permute-start(bf16[256,512]{1,0:T(8,128)(2,1)S(1)} %get-tuple-element.60), channel_id=1, source_target_pairs={{0,6},{1,7},{2,0},{3,1},{4,2},{5,3},{6,4},{7,5},{8,14},{9,15},{10,... | collective-permute-start | bytes 786440 | tf_op jit(solution)/shard_map/ppermute | solution.py:435
  159.4 22.1 %copy-start.14 = (f32[128,1]{1,0:T(8,128)S(1)}, f32[128,1]{1,0:T(8,128)}, u32[]{:S(2)}) copy-start(f32[128,1]{1,0:T(8,128)} %copy-done.13) | copy-start | bytes 1540
  180.3 33.3 %copy-start.12 = (s32[128,1,128]{2,1,0:T(1,128)S(1)}, s32[128,1,128]{2,1,0:T(1,128)}, u32[]{:S(2)}) copy-start(s32[128,1,128]{2,1,0:T(1,128)} %copy-done.11) | copy-start | bytes 196612
  180.3 21.4 %collective-permute-start.14 = (bf16[528,512]{1,0:T(8,128)(2,1)S(1)}, bf16[528,512]{1,0:T(8,128)(2,1)S(1)}, u32[]{:S(2)}, u32[]{:S(2)}) collective-permute-start(bf16[528,512]{1,0:T(8,128)(2,1)S(1)} %get-tuple-element.63), channel_id=1, source_target_pairs={{0,8},{1,9},{2,10},{3,11},{4,12},{5,13},{6,14},{7,15},{8,0},{9,1},... | collective-permute-start | bytes 1622024 | tf_op jit(solution)/shard_map/ppermute | solution.py:450
  181.5 21.1 %collective-permute-start.15 = (f32[128,1]{1,0:T(8,128)S(1)}, f32[128,1]{1,0:T(8,128)S(1)}, u32[]{:S(2)}, u32[]{:S(2)}) collective-permute-start(f32[128,1]{1,0:T(8,128)S(1)} %copy-done.14), channel_id=1, source_target_pairs={{0,128},{128,0},{1,129},{129,1},{2,130},{130,2},{3,131},{131,3},{4... | collective-permute-start | bytes 1544 | tf_op jit(solution)/shard_map/ppermute | solution.py:453
  202.6 30.7 %all-to-all-start.3 = ((bf16[64,40,128]{2,1,0:T(8,128)(2,1)}), bf16[64,40,128]{2,1,0:T(8,128)(2,1)S(1)}, u32[]{:S(2)}, u32[]{:S(2)}) async-start(bf16[64,40,128]{2,1,0:T(8,128)(2,1)} %bitcast.14), calls=%async_computation.3 | async-start | bytes 1310720 | tf_op jit(solution)/shard_map/all_to_all | solution.py:455
  (22 other events, 163.7 us)
